TPU v7x, 128 devices: a whole 4x4x4 slice. The times are simulated.
128 devices in a mesh: row: 16 (over z, y), col: 8 (over x, core).
Axes of the slice: x: 4, y: 4, z: 4, core: 2. Of those that a mesh axis runs over, the one named last changes fastest.
Arguments:
- amplitudes: bfloat16 [8192, 7680], P(('row', 'col')), may hold values from -6 to 6
- integrals: bfloat16 [8, 7680, 1920], P('col', 'row'), may hold values from -0.0625 to 0.0625
- tile_ids: int32 [80], replicated, may hold values from 0 to 42335, as said below
- tile_owner: int32 [80], replicated, may hold values from 0 to 7, as said below
- occ_pairs: int32 [8192, 2], replicated, may hold values from 0 to 199
- occ_energy: float32 [200], replicated, may hold values from -1 to -0.2
- vir_energy: float32 [2016], replicated, may hold values from 0.1 to 1.5
Outputs:
- ladder_update: float32 [16, 512, 7680], P('row', 'col')
Inputs may be any that keep to these rules, and one draw needn't show every extreme that they name: `tile_ids`: distinct; tile g covers the flat virtual pairs g * 96 to g * 96 + 95, flat pair f being the virtuals f // 2016 and f % 2016. `tile_owner`: every column owns at least one tile and at most 20, one column exactly 20; integral slots past a column's count are unused.
All inputs are finite; a program needn't handle non-finite values.
Results may differ from a plain program's by a relative error of at most 0.0003.
Values may be sent and summed in bfloat16 or wider, within the bound.
No kernel may reach another device: no remote copies, remote signals or barrier semaphores. Data moves between devices by JAX's collectives and lax.ppermute only.
A program may use at most 128 MiB of HBM per device.

v0:
```python
import functools

import jax
import jax.numpy as jnp
from jax import lax
from jax.experimental import pallas as pl
from jax.experimental.pallas import tpu as pltpu
from jax.sharding import Mesh, PartitionSpec as P

TW = 96
NVIR = 2016
SIDE = 4
TILES = 80
CAP = 20
QUAD = 4
LANES = 128
WINDOW = 2 * LANES
HALF = 240
PADDED = 256
WIDTH = CAP * TW
CUT = 128
LEVELS = 32000.0
STEPS = 256.0
ALL = ("z", "y", "x", "c")
SEND = 0
GATHER = 3 * CAP
ROUNDS = GATHER + CAP
VMEM = pltpu.CompilerParams(vmem_limit_bytes=48 * 1024 * 1024)


def ring(value, axis, shift):
    return lax.ppermute(value, axis, [(i, (i + shift) % SIDE) for i in range(SIDE)])


def part_ring(up, down, axis):
    value = up if up is down else jnp.where(lax.axis_index("c") == 0, up, down)
    pairs = [(2 * i + c, 2 * ((i + 1 - 2 * c) % SIDE) + c) for i in range(SIDE) for c in range(2)]
    return lax.ppermute(value, (axis, "c"), pairs)


def swap(value):
    return lax.ppermute(value, "c", [(0, 1), (1, 0)])


def four_tiles(load, starts, limit):
    parts = []
    for start, want in zip(starts, (0, 96, 64, 160)):
        base = jnp.minimum((start // LANES) * LANES, limit - WINDOW)
        window = load(pl.multiple_of(base, LANES))
        parts.append(pltpu.roll(window, (want - (start - base)) & (WINDOW - 1), 1))
    a, b, c, d = parts
    lane = lax.broadcasted_iota(jnp.int32, (a.shape[0], LANES), 1)
    return (
        jnp.where(lane < 96, a[:, :LANES], b[:, :LANES]),
        jnp.where(lane < 64, b[:, LANES:], c[:, :LANES]),
        jnp.where(lane < 32, c[:, LANES:], d[:, LANES:]),
    )


def one_hot(size, source):
    row = lax.broadcasted_iota(jnp.int32, (size, size), 0)
    col = lax.broadcasted_iota(jnp.int32, (size, size), 1)
    return jnp.where(col == source(row), 1.0, 0.0).astype(jnp.bfloat16)


def plan_kernel(owner, out):
    x, c = (lax.axis_index(name).astype(jnp.float32) for name in "xc")
    i = lax.broadcasted_iota(jnp.int32, (TILES, TILES), 0)
    j = lax.broadcasted_iota(jnp.int32, (TILES, TILES), 1)
    across = lambda mask, value=1.0: jnp.sum(jnp.where(mask, value, 0.0), axis=1, keepdims=True)
    down = lambda mask, value=1.0: jnp.sum(jnp.where(mask, value, 0.0), axis=0, keepdims=True)
    earlier = j < i
    owner_row = owner[...].astype(jnp.float32)
    owner_col = across(i == j, owner_row)
    home_row, home = jnp.floor(owner_row * 0.5), jnp.floor(owner_col * 0.5)
    slot = across((owner_row == owner_col) & earlier)
    rank = across((home_row == home) & earlier)
    moves = rank >= CAP
    over = under = jnp.zeros((1, 1), jnp.float32)
    number = rank - CAP
    ends, starts = [], []
    for k in range(SIDE):
        load = across(home_row == k)
        number = number + jnp.where(home == k, over, 0.0)
        starts.append(load - under)
        over = over + jnp.maximum(load - CAP, 0.0)
        under = under + jnp.maximum(CAP - load, 0.0)
        ends.append(under)
    target = jnp.where(moves, sum(jnp.where(number >= end, 1.0, 0.0) for end in ends), home)
    start = sum(jnp.where(target == k, starts[k], 0.0) for k in range(SIDE))
    pos = jnp.where(moves, start + number, rank)
    moving = jnp.where(moves, home * SIDE + target, -1.0)
    order = across((down(i == j, moving) == moving) & earlier)
    place = jnp.where(owner_col - 2.0 * home == c, slot, CAP + slot)
    shift = target - home
    shift = jnp.where(shift < 0.0, shift + SIDE, shift) - 1.0
    lane = lax.broadcasted_iota(jnp.int32, (TILES, LANES), 1).astype(jnp.float32)
    row = lax.broadcasted_iota(jnp.int32, (TILES, LANES), 0).astype(jnp.float32)
    perm = down(lane == target * CAP + pos, row)
    outgoing = jnp.where(moves & (home == x), SEND + shift * CAP + order, -1.0)
    group = jnp.floor(order * (1.0 / QUAD))
    arriving = 2 * CAP + group * 3 * QUAD + shift * QUAD + order - group * QUAD
    incoming = jnp.where(target == x, GATHER + pos, -1.0)
    table = down(lane == outgoing, place) + down(lane == incoming, jnp.where(moves, arriving, place))
    most = jnp.max(jnp.where(moves, order, -1.0), axis=0, keepdims=True)
    rounds = jnp.floor((most + QUAD) * (1.0 / QUAD))
    table = jnp.where(lane[:1] == ROUNDS, rounds, table)
    out[0:1, :] = perm.astype(jnp.int32)
    out[1:2, :] = table.astype(jnp.int32)


def make_plan(tile_owner):
    vmem = pl.BlockSpec(memory_space=pltpu.VMEM)
    return pl.pallas_call(
        plan_kernel,
        out_shape=jax.ShapeDtypeStruct((2, LANES), jnp.int32),
        in_specs=[vmem],
        out_specs=vmem,
        name="make_plan",
    )(tile_owner[None, :])


def amplitude_kernel(table, amp, after, *outs):
    x = lax.axis_index("x")
    load = lambda base: amp[:, pl.ds(base, WINDOW)].astype(jnp.float32)
    for s, out in enumerate(outs):
        first = ((x + s) % SIDE) * CAP

        def four(g, carry, first=first, out=out):
            starts = [table[0, first + QUAD * g + j] * TW for j in range(QUAD)]
            for k, column in enumerate(four_tiles(load, starts, TILES * TW)):
                at = pl.multiple_of(g * QUAD * TW + k * LANES, LANES)
                out[:, pl.ds(at, LANES)] = column.astype(jnp.bfloat16)
            return carry

        lax.fori_loop(0, CAP // QUAD, four, 0)


def order_amplitudes(table, amplitudes, after):
    vmem = pl.BlockSpec(memory_space=pltpu.VMEM)
    return pl.pallas_call(
        amplitude_kernel,
        out_shape=tuple(jax.ShapeDtypeStruct((64, WIDTH), jnp.bfloat16) for _ in range(SIDE)),
        in_specs=[pl.BlockSpec(memory_space=pltpu.SMEM), vmem, pl.BlockSpec(memory_space=pl.ANY)],
        out_specs=tuple(vmem for _ in range(SIDE)),
        compiler_params=VMEM,
        name="order_amplitudes",
    )(table, amplitudes, after)


def tile_rows(pool, table, first, out, at):
    def rows(i, carry):
        here = pl.ds(pl.multiple_of(i * 48, 16), 48)
        load = lambda base: pool[here, pl.ds(base, WINDOW)].astype(jnp.float32)
        starts = [table[1, first + j] * TW for j in range(QUAD)]
        for k, column in enumerate(four_tiles(load, starts, pool.shape[1])):
            out[here, pl.ds(pl.multiple_of(at + k * LANES, LANES), LANES)] = column.astype(jnp.bfloat16)
        return carry

    lax.fori_loop(0, HALF // 48, rows, 0)


def fill_pool(sources, pool, sems):
    half = pl.ds(pl.multiple_of(lax.axis_index("c") * HALF, 16), HALF)
    copies = []
    at = 0
    for i, ref in enumerate(sources):
        src = ref.at[half] if i < 2 else ref
        width = ref.shape[1]
        copies.append(pltpu.make_async_copy(src, pool.at[:, pl.ds(at, width)], sems.at[i]))
        at += width
    for copy in copies:
        copy.start()
    for copy in copies:
        copy.wait()


def pack_kernel(number, table, mine, other, after, out1, out2, out3, pool, sems):
    fill_pool((mine, other), pool, sems)
    for s, out in enumerate((out1, out2, out3)):
        tile_rows(pool, table, SEND + s * CAP + number * QUAD, out, 0)


def assemble_kernel(table, mine, other, in1, in2, in3, extra, out, pool, sems):
    fill_pool((mine, other, in1, in2, in3), pool, sems)
    at, width = 2 * WIDTH + 3 * QUAD * TW, QUAD * TW

    @pl.when(table[1, ROUNDS] > 1)
    def _():
        copies = [
            pltpu.make_async_copy(extra.at[i], pool.at[:, pl.ds(at + i * width, width)], sems.at[i])
            for i in range(extra.shape[0])
        ]
        for copy in copies:
            copy.start()
        for copy in copies:
            copy.wait()

    def four(g, carry):
        tile_rows(pool, table, GATHER + g * QUAD, out, g * QUAD * TW)
        return carry

    lax.fori_loop(0, CAP // QUAD, four, 0)


def pack(number, table, mine, other, after):
    anywhere = pl.BlockSpec(memory_space=pl.ANY)
    return pl.pallas_call(
        functools.partial(pack_kernel, number),
        out_shape=tuple(jax.ShapeDtypeStruct((HALF, QUAD * TW), jnp.bfloat16) for _ in range(3)),
        in_specs=[pl.BlockSpec(memory_space=pltpu.SMEM), anywhere, anywhere, anywhere],
        out_specs=tuple(pl.BlockSpec(memory_space=pltpu.VMEM) for _ in range(3)),
        scratch_shapes=[pltpu.VMEM((HALF, 2 * WIDTH), jnp.bfloat16), pltpu.SemaphoreType.DMA((2,))],
        compiler_params=VMEM,
        name="pack",
    )(table, mine, other, after)


def assemble(table, mine, other, received, extra):
    anywhere = pl.BlockSpec(memory_space=pl.ANY)
    n = len(received) + extra.shape[0]
    return pl.pallas_call(
        assemble_kernel,
        out_shape=jax.ShapeDtypeStruct((HALF, WIDTH), jnp.bfloat16),
        in_specs=[pl.BlockSpec(memory_space=pltpu.SMEM)] + [anywhere] * 6,
        out_specs=pl.BlockSpec(memory_space=pltpu.VMEM),
        scratch_shapes=[
            pltpu.VMEM((HALF, 2 * WIDTH + n * QUAD * TW), jnp.bfloat16),
            pltpu.SemaphoreType.DMA((2 + n,)),
        ],
        compiler_params=VMEM,
        cost_estimate=pl.CostEstimate(flops=0, bytes_accessed=10 << 20, transcendentals=0),
        name="assemble",
    )(table, mine, other, *received, extra)


def send(packed):
    return [ring(part, "x", s + 1) for s, part in enumerate(packed)]


def later_rounds(table, mine, other):
    def more(table, mine, other):
        parts = []
        for number in range(1, CAP // QUAD):
            parts += send(pack(number, table, mine, other, parts[-1] if parts else table))
        return jnp.stack(parts)

    def none(table, mine, other):
        return jnp.zeros((3 * (CAP // QUAD - 1), HALF, QUAD * TW), mine.dtype)

    return lax.cond(table[1, ROUNDS] > 1, more, none, table, mine, other)


def encode(value):
    top = jnp.max(jnp.abs(value), axis=1, keepdims=True)
    code = jnp.ceil(jnp.log2(jnp.maximum(top, 1e-33)) * STEPS)
    level = jnp.floor(value * (jnp.exp2(code * (-1.0 / STEPS)) * LEVELS) + 0.5)
    return level.astype(jnp.int32).astype(jnp.int16), code.astype(jnp.int32).astype(jnp.int16)


def decode(coded):
    wide = coded.astype(jnp.int32).astype(jnp.float32)
    lane = lax.broadcasted_iota(jnp.int32, wide.shape, 1)
    code = jnp.sum(jnp.where(lane == HALF, wide, 0.0), axis=1, keepdims=True)
    return wide[:, :HALF] * (jnp.exp2(code * (1.0 / STEPS)) * (1.0 / LEVELS))


def put(out, k, level, code):
    out[k, :, :HALF] = level
    out[k, :, HALF:] = jnp.broadcast_to(code, (64, PADDED - HALF))


def code_far_kernel(n, *refs):
    for k in range(n):
        put(refs[n], k, *encode(refs[k][...]))


def code_near_kernel(n, *refs):
    sums, (arrived, nxt, prv) = refs[: 2 * n], refs[2 * n :]
    c = lax.axis_index("c")

    def run(first, out, other_first, other_out):
        for k in range(n):
            put(out, k, *encode(sums[first + k][...] + decode(arrived[k])))
        for k in range(n):
            put(other_out, k, *encode(sums[other_first + k][...]))

    pl.when(c == 0)(lambda: run(0, nxt, n, prv))
    pl.when(c != 0)(lambda: run(n, prv, 0, nxt))


def code_last_kernel(n, *refs):
    sums, (low, high, _, out) = refs[:n], refs[n:]
    for k in range(n):
        level, code = encode(sums[k][...] + decode(low[k]) + decode(high[k]))
        code = jnp.broadcast_to(code, (64, PADDED - HALF))
        for row in range(SIDE):
            rows = slice(16 * row, 16 * (row + 1))
            out[row, k, :, :HALF] = level[rows]
            out[row, k, :, HALF:] = code[rows]


def code_far(sums):
    n = len(sums)
    return pl.pallas_call(
        functools.partial(code_far_kernel, n),
        out_shape=jax.ShapeDtypeStruct((n, 2 * CUT, PADDED), jnp.int16),
        grid=(4,),
        in_specs=[pl.BlockSpec((64, HALF), lambda i: (i, 0))] * n,
        out_specs=pl.BlockSpec((n, 64, PADDED), lambda i: (0, i, 0)),
        compiler_params=VMEM,
        name="code_far",
    )(*sums)


def code_near(sums_next, sums_prev, arrived):
    n = len(sums_next)
    out = jax.ShapeDtypeStruct((n, 2 * CUT, PADDED), jnp.int16)
    block = pl.BlockSpec((n, 64, PADDED), lambda i: (0, i, 0))
    return pl.pallas_call(
        functools.partial(code_near_kernel, n),
        out_shape=(out, out),
        grid=(4,),
        in_specs=[pl.BlockSpec((64, HALF), lambda i: (i, 0))] * (2 * n) + [block],
        out_specs=(block, block),
        compiler_params=VMEM,
        name="code_near",
    )(*sums_next, *sums_prev, arrived)


def code_last(sums, low, high, group, before):
    n = len(sums)
    block = pl.BlockSpec((n, 64, PADDED), lambda i: (0, i, 0))
    return pl.pallas_call(
        functools.partial(code_last_kernel, n),
        out_shape=jax.ShapeDtypeStruct((SIDE * SIDE, 2 * n, 16, PADDED), jnp.int16),
        grid=(4,),
        in_specs=[pl.BlockSpec((64, HALF), lambda i: (i, 0))] * n
        + [block, block, pl.BlockSpec(memory_space=pl.ANY)],
        out_specs=pl.BlockSpec((SIDE, n, 16, PADDED), lambda i: (i, group, 0, 0)),
        input_output_aliases={} if before is None else {n + 2: 0},
        compiler_params=VMEM,
        name="code_last",
    )(*sums, low, high, low if before is None else before)


def finish_kernel(groups, *refs):
    c = lax.axis_index("c")
    got, (virt, occ, out) = refs[: len(groups)], refs[len(groups) :]
    spots = {up: (ref, 2 * k) for ref, group in zip(got, groups) for k, up in enumerate(group)}
    by_zr = one_hot(64, lambda i: ((i // 4) % 4) * 16 + (i // 16) * 4 + i % 4).astype(jnp.float32)
    for ya in range(SIDE):
        for h in range(2):
            parts = []
            for ys in range(SIDE):
                ref, k = spots[(ya - ys) % SIDE]
                parts.append(ref[ys, k + jnp.bitwise_xor(c, h)])
            value = decode(jnp.concatenate(parts, axis=0))
            value = jnp.dot(by_zr, value, precision=lax.Precision.HIGHEST)
            j = 2 * ya + h
            out[:, j * HALF : (j + 1) * HALF] = value / (virt[j : j + 1, :HALF] - occ[...])


def finish(groups, got, virt, occ):
    block = lambda n: pl.BlockSpec((SIDE, n, 16, PADDED), lambda i: (i, 0, 0, 0))
    return pl.pallas_call(
        functools.partial(finish_kernel, groups),
        grid=(SIDE,),
        out_shape=jax.ShapeDtypeStruct((64, SIDE * WIDTH), jnp.float32),
        in_specs=[block(2 * len(group)) for group in groups]
        + [
            pl.BlockSpec((8, PADDED), lambda i: (i, 0)),
            pl.BlockSpec((64, 1), lambda i: (0, 0)),
        ],
        out_specs=pl.BlockSpec((64, WIDTH), lambda i: (0, i)),
        compiler_params=VMEM,
        name="finish",
    )(*got, virt, occ)


def ring_pieces(first, second):
    both = (first, second)
    steps = [ring(piece, axis, shift) for piece, axis, _ in both for shift in (1, -1)]
    steps = lax.optimization_barrier(tuple(steps))
    lows, highs = steps[0::2], steps[1::2]
    fars = []
    for (_, axis, cut), low, high in zip(both, lows, highs):
        fars += [ring(low[:cut], axis, 1), ring(high[cut:], axis, -1)]
    fars = lax.optimization_barrier(tuple(fars))
    return [
        (piece, high, *fars[2 * i : 2 * i + 2], low)
        for i, ((piece, _, _), low, high) in enumerate(zip(both, lows, highs))
    ]


def on_device(amplitudes, integrals, tile_ids, tile_owner, occ_pairs, occ_energy, vir_energy):
    z, y, x, c = (lax.axis_index(name) for name in ALL)
    occ_dev = amplitudes.shape[0]
    sub = occ_dev // (SIDE * SIDE)
    mine = integrals[0]
    other = swap(mine)
    table = make_plan(tile_owner)
    extra = later_rounds(table, mine, other)
    packed = pack(0, table, mine, other, extra)
    first = send(packed)
    last, *leaving = order_amplitudes(table, amplitudes, packed[0])
    prev, far, nxt = send(leaving)
    shard = assemble(table, mine, other, first, extra)
    arrived = jnp.concatenate([far, nxt, prev, last], axis=0)
    arrived, _ = lax.optimization_barrier((arrived, shard))
    shares, pieces = ring_pieces((shard, "y", CUT), (arrived, "z", 2 * occ_dev))
    own, high, far0, far1, low = [(piece, swap(piece)) for piece in shares]
    both = tuple(jnp.concatenate([far0[i], far1[i]], axis=0) for i in range(2))
    blocks = [own, high, both, low]
    by_k = one_hot(256, lambda i: (((i // 4) % 4 - z) % 4) * 64 + (i // 16) * 4 + i % 4)

    def pairs_of(number):
        own, high, far0, far1, low = pieces
        at = lambda p, n: p[n * occ_dev : (n + 1) * occ_dev]
        far = at(far0, number) if number < 2 else at(far1, number - 2)
        whole = jnp.concatenate([at(own, number), at(high, number), far, at(low, number)], axis=0)
        return jnp.dot(by_k, whole, preferred_element_type=jnp.float32).astype(whole.dtype)

    def product(a, b):
        return lax.dot_general(a, b, (((1,), (1,)), ((), ())), preferred_element_type=jnp.float32)

    def sums(number, blocks):
        return [product(pairs[number], b) for b in blocks]

    pairs = [pairs_of(number) for number in range(SIDE)]

    def near_sums(next_pairs, prev_pairs, *blocks):
        return [product(p, b) for p in (next_pairs, prev_pairs) for b in blocks]

    def no_sums(next_pairs, prev_pairs, *blocks):
        return [jnp.zeros((4 * occ_dev, HALF), jnp.float32) for _ in range(2 * len(blocks))]

    groups = ((0, 1), (2, 3))
    parts = [[half for up in group for half in blocks[up]] for group in groups]
    sent = [code_far(sums(0, part)) for part in parts]
    pairs[1], pairs[2], pairs[3], *_ = lax.optimization_barrier((*pairs[1:], *sent))
    far_sums = [part_ring(value, value, "x") for value in sent]
    leaving, behind = [], pairs[1:3]
    for part, arriving in zip(parts, far_sums):
        both = lax.cond(table[1, ROUNDS] >= 0, near_sums, no_sums, *behind, *part)
        leaving.append(code_near(both[: len(part)], both[len(part) :], arriving))
        *behind, _, _ = lax.optimization_barrier((pairs[1], pairs[2], *leaving[-1]))
    near_arrived = [(ring(nxt, "x", 1), ring(prv, "x", -1)) for nxt, prv in leaving]
    pairs[3], *_ = lax.optimization_barrier((pairs[3], *leaving[-1]))
    last_sums = [sums(3, part) for part in parts]
    total = None
    for group, (sums_, arriving) in enumerate(zip(last_sums, near_arrived)):
        total = code_last(sums_, *arriving, group, total)
    got = lax.all_to_all(total, ("z", "y"), split_axis=0, concat_axis=0, tiled=True)
    sent = leaving[-1]
    occ_pairs, occ_energy, vir_energy, _ = lax.optimization_barrier(
        (occ_pairs, occ_energy, vir_energy, sent[0])
    )

    grid = occ_pairs.reshape(SIDE * SIDE, 2 * SIDE, SIDE * SIDE, sub, 2)
    here = lax.dynamic_slice(grid, (0, 2 * x + c, SIDE * z + y, 0, 0), (SIDE * SIDE, 1, 1, sub, 2))
    occ_sum = jnp.sum(jnp.take(occ_energy, here.reshape(occ_dev, 2), axis=0), axis=1)
    per_row = NVIR // TW
    second = jnp.take(vir_energy.reshape(per_row, TW), tile_ids % per_row, axis=0)
    virt_sum = (jnp.take(vir_energy, tile_ids // per_row)[:, None] + second).reshape(8 * SIDE, HALF)
    virt_sum = jnp.pad(virt_sum, ((0, 0), (0, PADDED - HALF)))
    return finish(((0, 1, 2, 3),), (got,), virt_sum, occ_sum[:, None])[None]


def solution(mesh):
    chips = Mesh(mesh.devices.reshape(SIDE, SIDE, SIDE, 2), ALL)
    placed = (P(ALL, None), P(("x", "c"), ("z", "y"), None), P(), P(), P(), P(), P())
    return jax.shard_map(
        on_device, mesh=chips, in_specs=placed, out_specs=P(("z", "y"), ("x", "c"), None), check_vma=False
    )
```

profile of v0, /device:TPU:0, one launch (start us, length us, event | category | flops | bytes accessed | tf_op | source)
XLA Modules:
  0.0 162.2 jit_solution(12344452321337246937)
XLA Ops:
  2.3 1.9 %collective-permute-done.12.other = bf16[480,1920]{1,0:T(8,128)(2,1)} collective-permute-done((bf16[480,1920]{1,0:T(8,128)(2,1)}, bf16[480,1920]{1,0:T(8,128)(2,1)}, u32[]{:S(2)}, u32[]{:S(2)}) %collective-permute-start.12) | collective-permute-done | bytes 1843232 | tf_op jit(solution)/shard_map/ppermute | solution.py:42
  5.7 4.0 %pack.9 = (bf16[240,384]{1,0:T(8,128)(2,1)S(1)}, bf16[240,384]{1,0:T(8,128)(2,1)S(1)}, bf16[240,384]{1,0:T(8,128)(2,1)S(1)}) custom-call(s32[2,128]{1,0:T(2,128)S(1)} %make_plan.1.table, bf16[480,1920]{1,0:T(8,128)(2,1)} %bitcast.101, bf16[480,1920]{1,0:T(8,128)(2,1)} %collective-permute-done.12.other, bf16[12,240,384]{2,1,0:T(8,128)(2,1)} %get-tuple-element.237.after.extra), custom_call_target="tpu_custom_call" | custom-call | tf_op jit(solution)/shard_map/pack/pallas_call | solution.py:208
  11.3 3.0 %order_amplitudes.1 = (bf16[64,1920]{1,0:T(8,128)(2,1)S(1)}, bf16[64,1920]{1,0:T(8,128)(2,1)S(1)}, bf16[64,1920]{1,0:T(8,128)(2,1)S(1)}, bf16[64,1920]{1,0:T(8,128)(2,1)S(1)}) custom-call(s32[2,128]{1,0:T(2,128)S(1)} %make_plan.1.table, bf16[64,7680]{1,0:T(8,128)(2,1)S(1)} %copy-done.1, bf16[240,384]{1,0:T(8,128)(2,1)S(1)} %get-tuple-element.110.after), custom_call_target="tpu_custom_call" | custom-call | tf_op jit(solution)/shard_map/order_amplitudes/pallas_call | solution.py:141
  15.9 1.7 %collective-permute-start.14 = (bf16[64,1920]{1,0:T(8,128)(2,1)S(1)}, bf16[64,1920]{1,0:T(8,128)(2,1)S(1)}, u32[]{:S(2)}, u32[]{:S(2)}) collective-permute-start(bf16[64,1920]{1,0:T(8,128)(2,1)S(1)} %get-tuple-element.112), channel_id=1, source_target_pairs={{0,6},{2,0},{4,2},{6,4},{1,7},{3,1},{5,3},{7,5},{8,14},{10,8},{12,... | collective-permute-start | bytes 737288 | tf_op jit(solution)/shard_map/ppermute | solution.py:32
  19.1 2.0 %collective-permute-start.17 = (bf16[240,384]{1,0:T(8,128)(2,1)S(1)}, bf16[240,384]{1,0:T(8,128)(2,1)S(1)}, u32[]{:S(2)}, u32[]{:S(2)}) collective-permute-start(bf16[240,384]{1,0:T(8,128)(2,1)S(1)} %get-tuple-element.115), channel_id=1, source_target_pairs={{0,4},{2,6},{4,0},{6,2},{1,5},{3,7},{5,1},{7,3},{8,12},{10,14},{12... | collective-permute-start | bytes 552968 | tf_op jit(solution)/shard_map/ppermute | solution.py:32
  21.6 11.6 %collective-permute-done.17.in2 = bf16[240,384]{1,0:T(8,128)(2,1)S(1)} collective-permute-done((bf16[240,384]{1,0:T(8,128)(2,1)S(1)}, bf16[240,384]{1,0:T(8,128)(2,1)S(1)}, u32[]{:S(2)}, u32[]{:S(2)}) %collective-permute-start.17) | collective-permute-done | bytes 184352 | tf_op jit(solution)/shard_map/ppermute | solution.py:32
  33.2 3.3 %collective-permute-done.18.in3 = bf16[240,384]{1,0:T(8,128)(2,1)S(1)} collective-permute-done((bf16[240,384]{1,0:T(8,128)(2,1)S(1)}, bf16[240,384]{1,0:T(8,128)(2,1)S(1)}, u32[]{:S(2)}, u32[]{:S(2)}) %collective-permute-start.18) | collective-permute-done | bytes 184352 | tf_op jit(solution)/shard_map/ppermute | solution.py:32
  36.5 5.0 %assemble.1 = bf16[240,1920]{1,0:T(8,128)(2,1)S(1)} custom-call(s32[2,128]{1,0:T(2,128)S(1)} %make_plan.1.table, bf16[480,1920]{1,0:T(8,128)(2,1)S(1)} %bitcast.102, bf16[480,1920]{1,0:T(8,128)(2,1)} %collective-permute-done.12.other, bf16[240,384]{1,0:T(8,128)(2,1)S(1)} %collective-permute-done.16.in1, bf16[240,384]{1,0:T(8,128)(2,1)S(1)} %collective-permute-done.17.in2, ...), custom_call_target="tpu_custom_call" | custom-call | bytes 10485760 | tf_op jit(solution)/shard_map/assemble/pallas_call | solution.py:222
  41.6 2.0 %collective-permute-start.21 = (bf16[256,1920]{1,0:T(8,128)(2,1)S(1)}, bf16[256,1920]{1,0:T(8,128)(2,1)S(1)}, u32[]{:S(2)}, u32[]{:S(2)}) collective-permute-start(bf16[256,1920]{1,0:T(8,128)(2,1)S(1)} %pad_maximum_fusion), channel_id=1, source_target_pairs={{0,32},{32,64},{64,96},{96,0},{1,33},{33,65},{65,97},{97,1},{2,34}... | collective-permute-start | bytes 2949128 | tf_op jit(solution)/shard_map/ppermute | solution.py:32
  43.6 2.2 %collective-permute-start.22 = (bf16[256,1920]{1,0:T(8,128)(2,1)S(1)}, bf16[256,1920]{1,0:T(8,128)(2,1)}, u32[]{:S(2)}, u32[]{:S(2)}) collective-permute-start(bf16[256,1920]{1,0:T(8,128)(2,1)S(1)} %pad_maximum_fusion), channel_id=1, source_target_pairs={{0,96},{32,0},{64,32},{96,64},{1,97},{33,1},{65,33},{97,65},{2,98}... | collective-permute-start | bytes 2949128 | tf_op jit(solution)/shard_map/ppermute | solution.py:32
  46.5 1.6 %collective-permute-start.19 = (bf16[240,1920]{1,0:T(8,128)(2,1)S(1)}, bf16[240,1920]{1,0:T(8,128)(2,1)S(1)}, u32[]{:S(2)}, u32[]{:S(2)}) collective-permute-start(bf16[240,1920]{1,0:T(8,128)(2,1)S(1)} %assemble.1), channel_id=1, source_target_pairs={{0,8},{8,16},{16,24},{24,0},{1,9},{9,17},{17,25},{25,1},{2,10},{10... | collective-permute-start | bytes 2764808 | tf_op jit(solution)/shard_map/ppermute | solution.py:32
  48.1 1.7 %collective-permute-start.20 = (bf16[240,1920]{1,0:T(8,128)(2,1)S(1)}, bf16[240,1920]{1,0:T(8,128)(2,1)S(1)}, u32[]{:S(2)}, u32[]{:S(2)}) collective-permute-start(bf16[240,1920]{1,0:T(8,128)(2,1)S(1)} %assemble.1), channel_id=1, source_target_pairs={{0,24},{8,0},{16,8},{24,16},{1,25},{9,1},{17,9},{25,17},{2,26},{10... | collective-permute-start | bytes 2764808 | tf_op jit(solution)/shard_map/ppermute | solution.py:32
  50.0 18.5 %collective-permute-done.19 = bf16[240,1920]{1,0:T(8,128)(2,1)S(1)} collective-permute-done((bf16[240,1920]{1,0:T(8,128)(2,1)S(1)}, bf16[240,1920]{1,0:T(8,128)(2,1)S(1)}, u32[]{:S(2)}, u32[]{:S(2)}) %collective-permute-start.19) | collective-permute-done | bytes 921632 | tf_op jit(solution)/shard_map/ppermute | solution.py:32
  68.6 1.8 %collective-permute-start.23 = (bf16[128,1920]{1,0:T(8,128)(2,1)S(1)}, bf16[128,1920]{1,0:T(8,128)(2,1)S(1)}, u32[]{:S(2)}, u32[]{:S(2)}) collective-permute-start(bf16[128,1920]{1,0:T(8,128)(2,1)S(1)} %slice.68), channel_id=1, source_target_pairs={{0,8},{8,16},{16,24},{24,0},{1,9},{9,17},{17,25},{25,1},{2,10},{10... | collective-permute-start | bytes 1474568 | tf_op jit(solution)/shard_map/ppermute | solution.py:32
  70.5 1.7 %collective-permute-start.24 = (bf16[112,1920]{1,0:T(8,128)(2,1)S(1)}, bf16[112,1920]{1,0:T(8,128)(2,1)S(1)}, u32[]{:S(2)}, u32[]{:S(2)}) collective-permute-start(bf16[112,1920]{1,0:T(8,128)(2,1)S(1)} %slice.69), channel_id=1, source_target_pairs={{0,24},{8,0},{16,8},{24,16},{1,25},{9,1},{17,9},{25,17},{2,26},{10... | collective-permute-start | bytes 1290248 | tf_op jit(solution)/shard_map/ppermute | solution.py:32
  73.4 3.3 %collective-permute-start.26 = (bf16[128,1920]{1,0:T(8,128)(2,1)S(1)}, bf16[128,1920]{1,0:T(8,128)(2,1)S(1)}, u32[]{:S(2)}, u32[]{:S(2)}) collective-permute-start(bf16[128,1920]{1,0:T(8,128)(2,1)S(1)} %slice.71), channel_id=1, source_target_pairs={{0,96},{32,0},{64,32},{96,64},{1,97},{33,1},{65,33},{97,65},{2,98}... | collective-permute-start | bytes 1474568 | tf_op jit(solution)/shard_map/ppermute | solution.py:32
  80.7 2.9 %collective-permute-done.25 = bf16[128,1920]{1,0:T(8,128)(2,1)S(1)} collective-permute-done((bf16[128,1920]{1,0:T(8,128)(2,1)S(1)}, bf16[128,1920]{1,0:T(8,128)(2,1)S(1)}, u32[]{:S(2)}, u32[]{:S(2)}) %collective-permute-start.25) | collective-permute-done | bytes 491552 | tf_op jit(solution)/shard_map/ppermute | solution.py:32
  94.9 1.7 %convolution_convert_fusion.1 = bf16[256,1920]{1,0:T(8,128)(2,1)} fusion(bf16[64,1920]{1,0:T(8,128)(2,1)S(1)} %get-tuple-element.191, bf16[64,1920]{1,0:T(8,128)(2,1)S(1)} %get-tuple-element.194, bf16[64,1920]{1,0:T(8,128)(2,1)S(1)} %get-tuple-element.178, bf16[64,1920]{1,0:T(8,128)(2,1)S(1)} %get-tuple-element.174, s32[256]{0:T(256)S(1)} %get-tuple-element.196, ...), kind=kOutput, calls=%fused_computation.16 | convolution fusion | flops 258244608 | bytes 1972996 | tf_op jit(solution)/shard_map/dot_general | solution.py:422
  96.6 3.8 %conditional.4 = (f32[256,240]{1,0:T(8,128)S(1)}, f32[256,240]{1,0:T(8,128)S(1)}, f32[256,240]{1,0:T(8,128)S(1)}, f32[256,240]{1,0:T(8,128)S(1)}, f32[256,240]{1...) conditional(s32[]{:T(128)} %bitcast.15, () %tuple.41, ...), branch_computations={%region_2.3_spmd, %region_3.4_spmd} | conditional | flops 1887436800 | bytes 17203264 | solution.py:445
  101.2 2.9 %code_near.2 = (s16[4,256,256]{2,1,0:T(8,128)(2,1)S(1)}, s16[4,256,256]{2,1,0:T(8,128)(2,1)S(1)}) custom-call(f32[256,240]{1,0:T(8,128)S(1)} %get-tuple-element.155.refs_0_, f32[256,240]{1,0:T(8,128)S(1)} %get-tuple-element.156.refs_1_, f32[256,240]{1,0:T(8,128)S(1)} %get-tuple-element.157.refs_2_, f32[256,240]{1,0:T(8,128)} %copy-done.31, ...), custom_call_target="tpu_custom_call" | custom-call | tf_op jit(solution)/shard_map/code_near/pallas_call | solution.py:320
  104.2 2.9 %collective-permute-start.36 = (s16[4,256,256]{2,1,0:T(8,128)(2,1)S(1)}, s16[4,256,256]{2,1,0:T(8,128)(2,1)S(1)}, u32[]{:S(2)}, u32[]{:S(2)}) collective-permute-start(s16[4,256,256]{2,1,0:T(8,128)(2,1)S(1)} %get-tuple-element.137), channel_id=1, source_target_pairs={{0,2},{2,4},{4,6},{6,0},{1,3},{3,5},{5,7},{7,1},{8,10},{10,12},{12... | collective-permute-start | bytes 1572872 | tf_op jit(solution)/shard_map/ppermute | solution.py:32
  107.7 5.4 %conditional.5 = (f32[256,240]{1,0:T(8,128)S(1)}, f32[256,240]{1,0:T(8,128)S(1)}, f32[256,240]{1,0:T(8,128)S(1)}, f32[256,240]{1,0:T(8,128)S(1)}, f32[256,240]{1...) conditional(s32[]{:T(128)} %bitcast.15, () %tuple.40, ...), branch_computations={%region_4.5_spmd, %region_5.6_spmd} | conditional | flops 1887436800 | bytes 31948976 | solution.py:445
  107.7 1.8 %fusion.57 = f32[256,240]{1,0:T(8,128)S(1)} fusion(bf16[256,1920]{1,0:T(8,128)(2,1)S(1)} %get-tuple-element.59, bf16[240,1920]{1,0:T(8,128)(2,1)} %get-tuple-element.60), kind=kOutput, calls=%fused_computation.113 | convolution fusion | flops 235929600 | bytes 2150400 | tf_op jit(solution)/shard_map/cond | solution.py:445
  113.2 1.6 %code_near.3 = (s16[4,256,256]{2,1,0:T(8,128)(2,1)S(1)}, s16[4,256,256]{2,1,0:T(8,128)(2,1)S(1)}) custom-call(f32[256,240]{1,0:T(8,128)S(1)} %get-tuple-element.163.refs_0_, f32[256,240]{1,0:T(8,128)S(1)} %get-tuple-element.164.refs_1_, f32[256,240]{1,0:T(8,128)S(1)} %get-tuple-element.165.refs_2_, f32[256,240]{1,0:T(8,128)S(1)} %get-tuple-element.166.refs_3_, ...), custom_call_target="tpu_custom_call" | custom-call | tf_op jit(solution)/shard_map/code_near/pallas_call | solution.py:320
  118.1 1.8 %collective-permute-start.35 = (s16[4,256,256]{2,1,0:T(8,128)(2,1)S(1)}, s16[4,256,256]{2,1,0:T(8,128)(2,1)S(1)}, u32[]{:S(2)}, u32[]{:S(2)}) collective-permute-start(s16[4,256,256]{2,1,0:T(8,128)(2,1)S(1)} %get-tuple-element.150), channel_id=1, source_target_pairs={{0,6},{2,0},{4,2},{6,4},{1,7},{3,1},{5,3},{7,5},{8,14},{10,8},{12,... | collective-permute-start | bytes 1572872 | tf_op jit(solution)/shard_map/ppermute | solution.py:32
  122.6 2.4 %code_last.2.refs_6_ = s16[16,8,16,256]{3,2,1,0:T(8,128)(2,1)} custom-call(f32[256,240]{1,0:T(8,128)S(1)} %fusion.77.refs_0_, f32[256,240]{1,0:T(8,128)S(1)} %fusion.78.refs_1_, f32[256,240]{1,0:T(8,128)S(1)} %fusion.79.refs_2_, f32[256,240]{1,0:T(8,128)S(1)} %fusion.80.refs_3_, s16[4,256,256]{2,1,0:T(8,128)(2,1)S(1)} %collective-permute-done.36.refs_4_.refs_6_, ...), custom_call_target="tpu_custom_call" | custom-call | tf_op jit(solution)/shard_map/code_last/pallas_call | solution.py:334
  125.0 7.2 %collective-permute-done.34.refs_4_ = s16[4,256,256]{2,1,0:T(8,128)(2,1)S(1)} collective-permute-done((s16[4,256,256]{2,1,0:T(8,128)(2,1)S(1)}, s16[4,256,256]{2,1,0:T(8,128)(2,1)S(1)}, u32[]{:S(2)}, u32[]{:S(2)}) %collective-permute-start.34) | collective-permute-done | bytes 524320 | tf_op jit(solution)/shard_map/ppermute | solution.py:32
  132.2 2.4 %code_last.3 = s16[16,8,16,256]{3,2,1,0:T(8,128)(2,1)} custom-call(f32[256,240]{1,0:T(8,128)S(1)} %fusion.73.refs_0_, f32[256,240]{1,0:T(8,128)S(1)} %fusion.74.refs_1_, f32[256,240]{1,0:T(8,128)S(1)} %fusion.75.refs_2_, f32[256,240]{1,0:T(8,128)S(1)} %fusion.76.refs_3_, ...), custom_call_target="tpu_custom_call", output_to_operand_aliasing={{}: (6, {})} | custom-call | tf_op jit(solution)/shard_map/code_last/pallas_call | solution.py:334
  134.5 6.2 %all-to-all-start = ((s16[16,8,16,256]{3,2,1,0:T(8,128)(2,1)}), s16[16,8,16,256]{3,2,1,0:T(8,128)(2,1)S(1)}, u32[]{:S(2)}, u32[]{:S(2)}) async-start(s16[16,8,16,256]{3,2,1,0:T(8,128)(2,1)} %code_last.3), calls=%async_computation | async-start | bytes 2097152 | tf_op jit(solution)/shard_map/all_to_all | solution.py:454
  142.9 2.2 %reshape.76 = s32[16,8,16,4,2]{3,2,1,0,4:T(8,128)S(1)} reshape(s32[8192,2]{0,1:T(2,128)S(1)} %copy-done.33) | data formatting | bytes 131072 | tf_op jit(solution)/shard_map/reshape | solution.py:460
  147.3 11.0 %all-to-all-done.refs_0_ = s16[16,8,16,256]{3,2,1,0:T(8,128)(2,1)S(1)} async-done(((s16[16,8,16,256]{3,2,1,0:T(8,128)(2,1)}), s16[16,8,16,256]{3,2,1,0:T(8,128)(2,1)S(1)}, u32[]{:S(2)}, u32[]{:S(2)}) %all-to-all-start) | async-done | bytes 1048608 | tf_op jit(solution)/shard_map/all_to_all | solution.py:454
  158.3 3.9 %finish.1 = f32[64,7680]{1,0:T(8,128)} custom-call(s16[16,8,16,256]{3,2,1,0:T(8,128)(2,1)S(1)} %all-to-all-done.refs_0_, f32[32,256]{1,0:T(8,128)S(1)} %pad.4.refs_1_, f32[64,1]{1,0:T(8,128)S(1)} %broadcast_in_dim.55.refs_2_), custom_call_target="tpu_custom_call" | custom-call | tf_op jit(solution)/shard_map/finish/pallas_call | solution.py:366
  (181 shorter events, 45.2 us)
Async XLA Ops:
  0.0 145.5 %copy-start = (f32[200]{0:T(256)S(1)}, f32[200]{0:T(256)}, u32[]{:S(2)}) copy-start(f32[200]{0:T(256)} %param.18) | copy-start | bytes 2404
  0.0 4.1 %collective-permute-start.12 = (bf16[480,1920]{1,0:T(8,128)(2,1)}, bf16[480,1920]{1,0:T(8,128)(2,1)}, u32[]{:S(2)}, u32[]{:S(2)}) collective-permute-start(bf16[480,1920]{1,0:T(8,128)(2,1)} %bitcast.99), channel_id=1, source_target_pairs={{0,1},{1,0},{2,3},{3,2},{4,5},{5,4},{6,7},{7,6},{8,9},{9,8},{10,11... | collective-permute-start | bytes 5529608 | tf_op jit(solution)/shard_map/ppermute | solution.py:42
  5.7 30.9 %copy-start.2 = (bf16[1,480,1920]{2,1,0:T(8,128)(2,1)S(1)}, bf16[1,480,1920]{2,1,0:T(8,128)(2,1)}, u32[]{:S(2)}) copy-start(bf16[1,480,1920]{2,1,0:T(8,128)(2,1)} %param.14) | copy-start | bytes 5529604
  9.7 11.5 %collective-permute-start.16 = (bf16[240,384]{1,0:T(8,128)(2,1)S(1)}, bf16[240,384]{1,0:T(8,128)(2,1)S(1)}, u32[]{:S(2)}, u32[]{:S(2)}) collective-permute-start(bf16[240,384]{1,0:T(8,128)(2,1)S(1)} %get-tuple-element.110.after), channel_id=1, source_target_pairs={{0,2},{2,4},{4,6},{6,0},{1,3},{3,5},{5,7},{7,1},{8,10},{10,12},{12... | collective-permute-start | bytes 552968 | tf_op jit(solution)/shard_map/ppermute | solution.py:32
  14.3 27.2 %collective-permute-start.15 = (bf16[64,1920]{1,0:T(8,128)(2,1)S(1)}, bf16[64,1920]{1,0:T(8,128)(2,1)S(1)}, u32[]{:S(2)}, u32[]{:S(2)}) collective-permute-start(bf16[64,1920]{1,0:T(8,128)(2,1)S(1)} %get-tuple-element.113), channel_id=1, source_target_pairs={{0,2},{2,4},{4,6},{6,0},{1,3},{3,5},{5,7},{7,1},{8,10},{10,12},{12... | collective-permute-start | bytes 737288 | tf_op jit(solution)/shard_map/ppermute | solution.py:32
  15.9 25.7 %collective-permute-start.14 = (bf16[64,1920]{1,0:T(8,128)(2,1)S(1)}, bf16[64,1920]{1,0:T(8,128)(2,1)S(1)}, u32[]{:S(2)}, u32[]{:S(2)}) collective-permute-start(bf16[64,1920]{1,0:T(8,128)(2,1)S(1)} %get-tuple-element.112), channel_id=1, source_target_pairs={{0,6},{2,0},{4,2},{6,4},{1,7},{3,1},{5,3},{7,5},{8,14},{10,8},{12,... | collective-permute-start | bytes 737288 | tf_op jit(solution)/shard_map/ppermute | solution.py:32
  17.6 23.9 %collective-permute-start.13 = (bf16[64,1920]{1,0:T(8,128)(2,1)S(1)}, bf16[64,1920]{1,0:T(8,128)(2,1)S(1)}, u32[]{:S(2)}, u32[]{:S(2)}) collective-permute-start(bf16[64,1920]{1,0:T(8,128)(2,1)S(1)} %get-tuple-element.111), channel_id=1, source_target_pairs={{0,4},{2,6},{4,0},{6,2},{1,5},{3,7},{5,1},{7,3},{8,12},{10,14},{12... | collective-permute-start | bytes 737288 | tf_op jit(solution)/shard_map/ppermute | solution.py:32
  19.1 14.0 %collective-permute-start.17 = (bf16[240,384]{1,0:T(8,128)(2,1)S(1)}, bf16[240,384]{1,0:T(8,128)(2,1)S(1)}, u32[]{:S(2)}, u32[]{:S(2)}) collective-permute-start(bf16[240,384]{1,0:T(8,128)(2,1)S(1)} %get-tuple-element.115), channel_id=1, source_target_pairs={{0,4},{2,6},{4,0},{6,2},{1,5},{3,7},{5,1},{7,3},{8,12},{10,14},{12... | collective-permute-start | bytes 552968 | tf_op jit(solution)/shard_map/ppermute | solution.py:32
  21.2 15.4 %collective-permute-start.18 = (bf16[240,384]{1,0:T(8,128)(2,1)S(1)}, bf16[240,384]{1,0:T(8,128)(2,1)S(1)}, u32[]{:S(2)}, u32[]{:S(2)}) collective-permute-start(bf16[240,384]{1,0:T(8,128)(2,1)S(1)} %get-tuple-element.116), channel_id=1, source_target_pairs={{0,6},{2,0},{4,2},{6,4},{1,7},{3,1},{5,3},{7,5},{8,14},{10,8},{12,... | collective-permute-start | bytes 552968 | tf_op jit(solution)/shard_map/ppermute | solution.py:32
  41.5 43.3 %copy-start.10 = (bf16[240,1920]{1,0:T(8,128)(2,1)}, bf16[240,1920]{1,0:T(8,128)(2,1)S(1)}, u32[]{:S(2)}) copy-start(bf16[240,1920]{1,0:T(8,128)(2,1)S(1)} %assemble.1) | copy-start | bytes 2764804
  41.6 27.0 %collective-permute-start.21 = (bf16[256,1920]{1,0:T(8,128)(2,1)S(1)}, bf16[256,1920]{1,0:T(8,128)(2,1)S(1)}, u32[]{:S(2)}, u32[]{:S(2)}) collective-permute-start(bf16[256,1920]{1,0:T(8,128)(2,1)S(1)} %pad_maximum_fusion), channel_id=1, source_target_pairs={{0,32},{32,64},{64,96},{96,0},{1,33},{33,65},{65,97},{97,1},{2,34}... | collective-permute-start | bytes 2949128 | tf_op jit(solution)/shard_map/ppermute | solution.py:32
  43.6 25.0 %collective-permute-start.22 = (bf16[256,1920]{1,0:T(8,128)(2,1)S(1)}, bf16[256,1920]{1,0:T(8,128)(2,1)}, u32[]{:S(2)}, u32[]{:S(2)}) collective-permute-start(bf16[256,1920]{1,0:T(8,128)(2,1)S(1)} %pad_maximum_fusion), channel_id=1, source_target_pairs={{0,96},{32,0},{64,32},{96,64},{1,97},{33,1},{65,33},{97,65},{2,98}... | collective-permute-start | bytes 2949128 | tf_op jit(solution)/shard_map/ppermute | solution.py:32
  46.5 22.1 %collective-permute-start.19 = (bf16[240,1920]{1,0:T(8,128)(2,1)S(1)}, bf16[240,1920]{1,0:T(8,128)(2,1)S(1)}, u32[]{:S(2)}, u32[]{:S(2)}) collective-permute-start(bf16[240,1920]{1,0:T(8,128)(2,1)S(1)} %assemble.1), channel_id=1, source_target_pairs={{0,8},{8,16},{16,24},{24,0},{1,9},{9,17},{17,25},{25,1},{2,10},{10... | collective-permute-start | bytes 2764808 | tf_op jit(solution)/shard_map/ppermute | solution.py:32
  48.1 20.4 %collective-permute-start.20 = (bf16[240,1920]{1,0:T(8,128)(2,1)S(1)}, bf16[240,1920]{1,0:T(8,128)(2,1)S(1)}, u32[]{:S(2)}, u32[]{:S(2)}) collective-permute-start(bf16[240,1920]{1,0:T(8,128)(2,1)S(1)} %assemble.1), channel_id=1, source_target_pairs={{0,24},{8,0},{16,8},{24,16},{1,25},{9,1},{17,9},{25,17},{2,26},{10... | collective-permute-start | bytes 2764808 | tf_op jit(solution)/shard_map/ppermute | solution.py:32
  49.8 37.6 %collective-permute-start.27 = (bf16[240,1920]{1,0:T(8,128)(2,1)S(1)}, bf16[240,1920]{1,0:T(8,128)(2,1)S(1)}, u32[]{:S(2)}, u32[]{:S(2)}) collective-permute-start(bf16[240,1920]{1,0:T(8,128)(2,1)S(1)} %assemble.1), channel_id=1, source_target_pairs={{0,1},{1,0},{2,3},{3,2},{4,5},{5,4},{6,7},{7,6},{8,9},{9,8},{10,11... | collective-permute-start | bytes 2764808 | tf_op jit(solution)/shard_map/ppermute | solution.py:42
  68.6 17.8 %copy-start.13 = (bf16[240,1920]{1,0:T(8,128)(2,1)}, bf16[240,1920]{1,0:T(8,128)(2,1)S(1)}, u32[]{:S(2)}) copy-start(bf16[240,1920]{1,0:T(8,128)(2,1)S(1)} %collective-permute-done.19) | copy-start | bytes 2764804
  68.6 28.0 %copy-start.22 = (bf16[240,1920]{1,0:T(8,128)(2,1)}, bf16[240,1920]{1,0:T(8,128)(2,1)S(1)}, u32[]{:S(2)}) copy-start(bf16[240,1920]{1,0:T(8,128)(2,1)S(1)} %collective-permute-done.20) | copy-start | bytes 2764804
  68.6 12.1 %collective-permute-start.23 = (bf16[128,1920]{1,0:T(8,128)(2,1)S(1)}, bf16[128,1920]{1,0:T(8,128)(2,1)S(1)}, u32[]{:S(2)}, u32[]{:S(2)}) collective-permute-start(bf16[128,1920]{1,0:T(8,128)(2,1)S(1)} %slice.68), channel_id=1, source_target_pairs={{0,8},{8,16},{16,24},{24,0},{1,9},{9,17},{17,25},{25,1},{2,10},{10... | collective-permute-start | bytes 1474568 | tf_op jit(solution)/shard_map/ppermute | solution.py:32
  70.5 8.9 %collective-permute-start.24 = (bf16[112,1920]{1,0:T(8,128)(2,1)S(1)}, bf16[112,1920]{1,0:T(8,128)(2,1)S(1)}, u32[]{:S(2)}, u32[]{:S(2)}) collective-permute-start(bf16[112,1920]{1,0:T(8,128)(2,1)S(1)} %slice.69), channel_id=1, source_target_pairs={{0,24},{8,0},{16,8},{24,16},{1,25},{9,1},{17,9},{25,17},{2,26},{10... | collective-permute-start | bytes 1290248 | tf_op jit(solution)/shard_map/ppermute | solution.py:32
  72.3 11.4 %collective-permute-start.25 = (bf16[128,1920]{1,0:T(8,128)(2,1)S(1)}, bf16[128,1920]{1,0:T(8,128)(2,1)S(1)}, u32[]{:S(2)}, u32[]{:S(2)}) collective-permute-start(bf16[128,1920]{1,0:T(8,128)(2,1)S(1)} %slice.70), channel_id=1, source_target_pairs={{0,32},{32,64},{64,96},{96,0},{1,33},{33,65},{65,97},{97,1},{2,34}... | collective-permute-start | bytes 1474568 | tf_op jit(solution)/shard_map/ppermute | solution.py:32
  73.4 10.6 %collective-permute-start.26 = (bf16[128,1920]{1,0:T(8,128)(2,1)S(1)}, bf16[128,1920]{1,0:T(8,128)(2,1)S(1)}, u32[]{:S(2)}, u32[]{:S(2)}) collective-permute-start(bf16[128,1920]{1,0:T(8,128)(2,1)S(1)} %slice.71), channel_id=1, source_target_pairs={{0,96},{32,0},{64,32},{96,64},{1,97},{33,1},{65,33},{97,65},{2,98}... | collective-permute-start | bytes 1474568 | tf_op jit(solution)/shard_map/ppermute | solution.py:32
  79.4 9.3 %collective-permute-start.28 = (bf16[240,1920]{1,0:T(8,128)(2,1)S(1)}, bf16[240,1920]{1,0:T(8,128)(2,1)S(1)}, u32[]{:S(2)}, u32[]{:S(2)}) collective-permute-start(bf16[240,1920]{1,0:T(8,128)(2,1)S(1)} %collective-permute-done.20), channel_id=1, source_target_pairs={{0,1},{1,0},{2,3},{3,2},{4,5},{5,4},{6,7},{7,6},{8,9},{9,8},{10,11... | collective-permute-start | bytes 2764808 | tf_op jit(solution)/shard_map/ppermute | solution.py:42
  80.7 10.5 %collective-permute-start.31 = (bf16[240,1920]{1,0:T(8,128)(2,1)S(1)}, bf16[240,1920]{1,0:T(8,128)(2,1)S(1)}, u32[]{:S(2)}, u32[]{:S(2)}) collective-permute-start(bf16[240,1920]{1,0:T(8,128)(2,1)S(1)} %collective-permute-done.19), channel_id=1, source_target_pairs={{0,1},{1,0},{2,3},{3,2},{4,5},{5,4},{6,7},{7,6},{8,9},{9,8},{10,11... | collective-permute-start | bytes 2764808 | tf_op jit(solution)/shard_map/ppermute | solution.py:42
  85.8 5.9 %collective-permute-start.29 = (bf16[128,1920]{1,0:T(8,128)(2,1)S(1)}, bf16[128,1920]{1,0:T(8,128)(2,1)S(1)}, u32[]{:S(2)}, u32[]{:S(2)}) collective-permute-start(bf16[128,1920]{1,0:T(8,128)(2,1)S(1)} %collective-permute-done.23), channel_id=1, source_target_pairs={{0,1},{1,0},{2,3},{3,2},{4,5},{5,4},{6,7},{7,6},{8,9},{9,8},{10,11... | collective-permute-start | bytes 1474568 | tf_op jit(solution)/shard_map/ppermute | solution.py:42
  85.9 5.9 %collective-permute-start.30 = (bf16[112,1920]{1,0:T(8,128)(2,1)S(1)}, bf16[112,1920]{1,0:T(8,128)(2,1)S(1)}, u32[]{:S(2)}, u32[]{:S(2)}) collective-permute-start(bf16[112,1920]{1,0:T(8,128)(2,1)S(1)} %collective-permute-done.24), channel_id=1, source_target_pairs={{0,1},{1,0},{2,3},{3,2},{4,5},{5,4},{6,7},{7,6},{8,9},{9,8},{10,11... | collective-permute-start | bytes 1290248 | tf_op jit(solution)/shard_map/ppermute | solution.py:42
  90.0 10.5 %collective-permute-start.32 = (s16[4,256,256]{2,1,0:T(8,128)(2,1)S(1)}, s16[4,256,256]{2,1,0:T(8,128)(2,1)S(1)}, u32[]{:S(2)}, u32[]{:S(2)}) collective-permute-start(s16[4,256,256]{2,1,0:T(8,128)(2,1)S(1)} %code_far.2), channel_id=1, source_target_pairs={{0,2},{1,7},{2,4},{3,1},{4,6},{5,3},{6,0},{7,5},{8,10},{9,15},{10,... | collective-permute-start | bytes 1572872 | tf_op jit(solution)/shard_map/ppermute | solution.py:38
  93.5 19.6 %collective-permute-start.33 = (s16[4,256,256]{2,1,0:T(8,128)(2,1)S(1)}, s16[4,256,256]{2,1,0:T(8,128)(2,1)S(1)}, u32[]{:S(2)}, u32[]{:S(2)}) collective-permute-start(s16[4,256,256]{2,1,0:T(8,128)(2,1)S(1)} %code_far.3), channel_id=1, source_target_pairs={{0,2},{1,7},{2,4},{3,1},{4,6},{5,3},{6,0},{7,5},{8,10},{9,15},{10,... | collective-permute-start | bytes 1572872 | tf_op jit(solution)/shard_map/ppermute | solution.py:38
  104.2 18.4 %collective-permute-start.36 = (s16[4,256,256]{2,1,0:T(8,128)(2,1)S(1)}, s16[4,256,256]{2,1,0:T(8,128)(2,1)S(1)}, u32[]{:S(2)}, u32[]{:S(2)}) collective-permute-start(s16[4,256,256]{2,1,0:T(8,128)(2,1)S(1)} %get-tuple-element.137), channel_id=1, source_target_pairs={{0,2},{2,4},{4,6},{6,0},{1,3},{3,5},{5,7},{7,1},{8,10},{10,12},{12... | collective-permute-start | bytes 1572872 | tf_op jit(solution)/shard_map/ppermute | solution.py:32
  107.1 15.5 %collective-permute-start.37 = (s16[4,256,256]{2,1,0:T(8,128)(2,1)S(1)}, s16[4,256,256]{2,1,0:T(8,128)(2,1)S(1)}, u32[]{:S(2)}, u32[]{:S(2)}) collective-permute-start(s16[4,256,256]{2,1,0:T(8,128)(2,1)S(1)} %get-tuple-element.138), channel_id=1, source_target_pairs={{0,6},{2,0},{4,2},{6,4},{1,7},{3,1},{5,3},{7,5},{8,14},{10,8},{12,... | collective-permute-start | bytes 1572872 | tf_op jit(solution)/shard_map/ppermute | solution.py:32
  116.6 15.6 %collective-permute-start.34 = (s16[4,256,256]{2,1,0:T(8,128)(2,1)S(1)}, s16[4,256,256]{2,1,0:T(8,128)(2,1)S(1)}, u32[]{:S(2)}, u32[]{:S(2)}) collective-permute-start(s16[4,256,256]{2,1,0:T(8,128)(2,1)S(1)} %get-tuple-element.149), channel_id=1, source_target_pairs={{0,2},{2,4},{4,6},{6,0},{1,3},{3,5},{5,7},{7,1},{8,10},{10,12},{12... | collective-permute-start | bytes 1572872 | tf_op jit(solution)/shard_map/ppermute | solution.py:32
  118.1 14.1 %collective-permute-start.35 = (s16[4,256,256]{2,1,0:T(8,128)(2,1)S(1)}, s16[4,256,256]{2,1,0:T(8,128)(2,1)S(1)}, u32[]{:S(2)}, u32[]{:S(2)}) collective-permute-start(s16[4,256,256]{2,1,0:T(8,128)(2,1)S(1)} %get-tuple-element.150), channel_id=1, source_target_pairs={{0,6},{2,0},{4,2},{6,4},{1,7},{3,1},{5,3},{7,5},{8,14},{10,8},{12,... | collective-permute-start | bytes 1572872 | tf_op jit(solution)/shard_map/ppermute | solution.py:32
  134.5 23.8 %all-to-all-start = ((s16[16,8,16,256]{3,2,1,0:T(8,128)(2,1)}), s16[16,8,16,256]{3,2,1,0:T(8,128)(2,1)S(1)}, u32[]{:S(2)}, u32[]{:S(2)}) async-start(s16[16,8,16,256]{3,2,1,0:T(8,128)(2,1)} %code_last.3), calls=%async_computation | async-start | bytes 2097152 | tf_op jit(solution)/shard_map/all_to_all | solution.py:454
  (29 other events, 106.2 us)
where the time goes:
time: 163 us; the launch traced here: 162 us
  waiting for transfers between devices  59.4 us (36%)
  starting transfers between devices  38.9 us (24%)
  Pallas kernels  27.8 us (17%)
  matrix products  20.1 us (12%)
  local copies, waits for them, and re-layouts  13.4 us (8%)
  between operations  2.11 us (1%)
    ppermute x18, waiting for transfers between devices, ring(): lax.ppermute(value, axis, [(i, (i + shift) % SIDE) for i in range(SIDE)])  46.5 us
    ppermute x18, starting transfers between devices, ring(): lax.ppermute(value, axis, [(i, (i + shift) % SIDE) for i in range(SIDE)])  30.2 us
    all_to_all x1, waiting for transfers between devices, on_device(): lax.all_to_all(total, ('z', 'y'), split_axis=0, concat_axis=0, tiled=True)  11 us
    cond x16, matrix products, on_device(): both = lax.cond(table[1, ROUNDS] >= 0, near_sums, no_sums, *behind, *part)  8.82 us
    dot_general x16, matrix products, product(): lax.dot_general(a, b, (((1,), (1,)), ((), ())), preferred_element_type=jn...  7.48 us
    all_to_all x1, starting transfers between devices, on_device(): lax.all_to_all(total, ('z', 'y'), split_axis=0, concat_axis=0, tiled=True)  6.24 us
    pallas_call x1, Pallas kernels, assemble(): pl.pallas_call(assemble_kernel, out_shape=jax.ShapeDtypeStruct((HALF, WID...  4.96 us
    pallas_call x2, Pallas kernels, code_last(): pl.pallas_call(functools.partial(code_last_kernel, n), out_shape=jax.Shap...  4.75 us
  transfers between devices with their start and end apart: 27, of which 10 were waited for; matrix products, arithmetic and copies ran while one was open for 19% of the time, Pallas kernels for 11%

commit v1 on v0

--- a/solution.py
+++ b/solution.py
@@ -246,7 +246,12 @@
         return jnp.stack(parts)
 
     def none(table, mine, other):
-        return jnp.zeros((3 * (CAP // QUAD - 1), HALF, QUAD * TW), mine.dtype)
+        return pl.pallas_call(
+            lambda out: None,
+            out_shape=jax.ShapeDtypeStruct((3 * (CAP // QUAD - 1), HALF, QUAD * TW), mine.dtype),
+            out_specs=pl.BlockSpec(memory_space=pl.ANY),
+            name="unused",
+        )()
 
     return lax.cond(table[1, ROUNDS] > 1, more, none, table, mine, other)
 

time: 163 us -> 161 us (0.988)
  no operation moved by 1% of the time
where the time goes in v1:
time: 161 us
  waiting for transfers between devices  59.4 us (37%)
  starting transfers between devices  38.9 us (24%)
  Pallas kernels  27.8 us (17%)
  matrix products  20.1 us (12%)
  local copies, waits for them, and re-layouts  11.9 us (7%)
  between operations  2.11 us (1%)
    ppermute x18, waiting for transfers between devices, ring(): lax.ppermute(value, axis, [(i, (i + shift) % SIDE) for i in range(SIDE)])  46.5 us
    ppermute x18, starting transfers between devices, ring(): lax.ppermute(value, axis, [(i, (i + shift) % SIDE) for i in range(SIDE)])  30.2 us
    all_to_all x1, waiting for transfers between devices, on_device(): lax.all_to_all(total, ('z', 'y'), split_axis=0, concat_axis=0, tiled=True)  11 us
    cond x16, matrix products, on_device(): both = lax.cond(table[1, ROUNDS] >= 0, near_sums, no_sums, *behind, *part)  8.82 us
    dot_general x16, matrix products, product(): lax.dot_general(a, b, (((1,), (1,)), ((), ())), preferred_element_type=jn...  7.48 us
    all_to_all x1, starting transfers between devices, on_device(): lax.all_to_all(total, ('z', 'y'), split_axis=0, concat_axis=0, tiled=True)  6.24 us
    pallas_call x1, Pallas kernels, assemble(): pl.pallas_call(assemble_kernel, out_shape=jax.ShapeDtypeStruct((HALF, WID...  4.96 us
    pallas_call x2, Pallas kernels, code_last(): pl.pallas_call(functools.partial(code_last_kernel, n), out_shape=jax.Shap...  4.75 us
  transfers between devices with their start and end apart: 27, of which 10 were waited for; matrix products, arithmetic and copies ran while one was open for 19% of the time, Pallas kernels for 11%

profile of v1, /device:TPU:0, one launch (start us, length us, event | category | flops | bytes accessed | tf_op | source)
XLA Modules:
  0.0 160.6 jit_solution(9094246497568145204)
XLA Ops:
  2.3 1.9 %collective-permute-done.12.other = bf16[480,1920]{1,0:T(8,128)(2,1)} collective-permute-done((bf16[480,1920]{1,0:T(8,128)(2,1)}, bf16[480,1920]{1,0:T(8,128)(2,1)}, u32[]{:S(2)}, u32[]{:S(2)}) %collective-permute-start.12) | collective-permute-done | bytes 1843232 | tf_op jit(solution)/shard_map/ppermute | solution.py:42
  4.1 4.0 %pack.9 = (bf16[240,384]{1,0:T(8,128)(2,1)S(1)}, bf16[240,384]{1,0:T(8,128)(2,1)S(1)}, bf16[240,384]{1,0:T(8,128)(2,1)S(1)}) custom-call(s32[2,128]{1,0:T(2,128)S(1)} %make_plan.1.table, bf16[480,1920]{1,0:T(8,128)(2,1)} %bitcast.101, bf16[480,1920]{1,0:T(8,128)(2,1)} %collective-permute-done.12.other, bf16[12,240,384]{2,1,0:T(8,128)(2,1)} %get-tuple-element.237.after.extra), custom_call_target="tpu_custom_call" | custom-call | tf_op jit(solution)/shard_map/pack/pallas_call | solution.py:208
  9.8 3.0 %order_amplitudes.1 = (bf16[64,1920]{1,0:T(8,128)(2,1)S(1)}, bf16[64,1920]{1,0:T(8,128)(2,1)S(1)}, bf16[64,1920]{1,0:T(8,128)(2,1)S(1)}, bf16[64,1920]{1,0:T(8,128)(2,1)S(1)}) custom-call(s32[2,128]{1,0:T(2,128)S(1)} %make_plan.1.table, bf16[64,7680]{1,0:T(8,128)(2,1)S(1)} %copy-done.1, bf16[240,384]{1,0:T(8,128)(2,1)S(1)} %get-tuple-element.110.after), custom_call_target="tpu_custom_call" | custom-call | tf_op jit(solution)/shard_map/order_amplitudes/pallas_call | solution.py:141
  14.3 1.7 %collective-permute-start.14 = (bf16[64,1920]{1,0:T(8,128)(2,1)S(1)}, bf16[64,1920]{1,0:T(8,128)(2,1)S(1)}, u32[]{:S(2)}, u32[]{:S(2)}) collective-permute-start(bf16[64,1920]{1,0:T(8,128)(2,1)S(1)} %get-tuple-element.112), channel_id=1, source_target_pairs={{0,6},{2,0},{4,2},{6,4},{1,7},{3,1},{5,3},{7,5},{8,14},{10,8},{12,... | collective-permute-start | bytes 737288 | tf_op jit(solution)/shard_map/ppermute | solution.py:32
  17.6 2.0 %collective-permute-start.17 = (bf16[240,384]{1,0:T(8,128)(2,1)S(1)}, bf16[240,384]{1,0:T(8,128)(2,1)S(1)}, u32[]{:S(2)}, u32[]{:S(2)}) collective-permute-start(bf16[240,384]{1,0:T(8,128)(2,1)S(1)} %get-tuple-element.115), channel_id=1, source_target_pairs={{0,4},{2,6},{4,0},{6,2},{1,5},{3,7},{5,1},{7,3},{8,12},{10,14},{12... | collective-permute-start | bytes 552968 | tf_op jit(solution)/shard_map/ppermute | solution.py:32
  20.1 11.6 %collective-permute-done.17.in2 = bf16[240,384]{1,0:T(8,128)(2,1)S(1)} collective-permute-done((bf16[240,384]{1,0:T(8,128)(2,1)S(1)}, bf16[240,384]{1,0:T(8,128)(2,1)S(1)}, u32[]{:S(2)}, u32[]{:S(2)}) %collective-permute-start.17) | collective-permute-done | bytes 184352 | tf_op jit(solution)/shard_map/ppermute | solution.py:32
  31.7 3.3 %collective-permute-done.18.in3 = bf16[240,384]{1,0:T(8,128)(2,1)S(1)} collective-permute-done((bf16[240,384]{1,0:T(8,128)(2,1)S(1)}, bf16[240,384]{1,0:T(8,128)(2,1)S(1)}, u32[]{:S(2)}, u32[]{:S(2)}) %collective-permute-start.18) | collective-permute-done | bytes 184352 | tf_op jit(solution)/shard_map/ppermute | solution.py:32
  35.0 5.0 %assemble.1 = bf16[240,1920]{1,0:T(8,128)(2,1)S(1)} custom-call(s32[2,128]{1,0:T(2,128)S(1)} %make_plan.1.table, bf16[480,1920]{1,0:T(8,128)(2,1)S(1)} %bitcast.102, bf16[480,1920]{1,0:T(8,128)(2,1)} %collective-permute-done.12.other, bf16[240,384]{1,0:T(8,128)(2,1)S(1)} %collective-permute-done.16.in1, bf16[240,384]{1,0:T(8,128)(2,1)S(1)} %collective-permute-done.17.in2, ...), custom_call_target="tpu_custom_call" | custom-call | bytes 10485760 | tf_op jit(solution)/shard_map/assemble/pallas_call | solution.py:222
  40.1 2.0 %collective-permute-start.21 = (bf16[256,1920]{1,0:T(8,128)(2,1)S(1)}, bf16[256,1920]{1,0:T(8,128)(2,1)S(1)}, u32[]{:S(2)}, u32[]{:S(2)}) collective-permute-start(bf16[256,1920]{1,0:T(8,128)(2,1)S(1)} %pad_maximum_fusion), channel_id=1, source_target_pairs={{0,32},{32,64},{64,96},{96,0},{1,33},{33,65},{65,97},{97,1},{2,34}... | collective-permute-start | bytes 2949128 | tf_op jit(solution)/shard_map/ppermute | solution.py:32
  42.1 2.2 %collective-permute-start.22 = (bf16[256,1920]{1,0:T(8,128)(2,1)S(1)}, bf16[256,1920]{1,0:T(8,128)(2,1)}, u32[]{:S(2)}, u32[]{:S(2)}) collective-permute-start(bf16[256,1920]{1,0:T(8,128)(2,1)S(1)} %pad_maximum_fusion), channel_id=1, source_target_pairs={{0,96},{32,0},{64,32},{96,64},{1,97},{33,1},{65,33},{97,65},{2,98}... | collective-permute-start | bytes 2949128 | tf_op jit(solution)/shard_map/ppermute | solution.py:32
  45.0 1.6 %collective-permute-start.19 = (bf16[240,1920]{1,0:T(8,128)(2,1)S(1)}, bf16[240,1920]{1,0:T(8,128)(2,1)S(1)}, u32[]{:S(2)}, u32[]{:S(2)}) collective-permute-start(bf16[240,1920]{1,0:T(8,128)(2,1)S(1)} %assemble.1), channel_id=1, source_target_pairs={{0,8},{8,16},{16,24},{24,0},{1,9},{9,17},{17,25},{25,1},{2,10},{10... | collective-permute-start | bytes 2764808 | tf_op jit(solution)/shard_map/ppermute | solution.py:32
  46.6 1.7 %collective-permute-start.20 = (bf16[240,1920]{1,0:T(8,128)(2,1)S(1)}, bf16[240,1920]{1,0:T(8,128)(2,1)S(1)}, u32[]{:S(2)}, u32[]{:S(2)}) collective-permute-start(bf16[240,1920]{1,0:T(8,128)(2,1)S(1)} %assemble.1), channel_id=1, source_target_pairs={{0,24},{8,0},{16,8},{24,16},{1,25},{9,1},{17,9},{25,17},{2,26},{10... | collective-permute-start | bytes 2764808 | tf_op jit(solution)/shard_map/ppermute | solution.py:32
  48.5 18.5 %collective-permute-done.19 = bf16[240,1920]{1,0:T(8,128)(2,1)S(1)} collective-permute-done((bf16[240,1920]{1,0:T(8,128)(2,1)S(1)}, bf16[240,1920]{1,0:T(8,128)(2,1)S(1)}, u32[]{:S(2)}, u32[]{:S(2)}) %collective-permute-start.19) | collective-permute-done | bytes 921632 | tf_op jit(solution)/shard_map/ppermute | solution.py:32
  67.1 1.6 %collective-permute-start.23 = (bf16[128,1920]{1,0:T(8,128)(2,1)S(1)}, bf16[128,1920]{1,0:T(8,128)(2,1)S(1)}, u32[]{:S(2)}, u32[]{:S(2)}) collective-permute-start(bf16[128,1920]{1,0:T(8,128)(2,1)S(1)} %slice.68), channel_id=1, source_target_pairs={{0,8},{8,16},{16,24},{24,0},{1,9},{9,17},{17,25},{25,1},{2,10},{10... | collective-permute-start | bytes 1474568 | tf_op jit(solution)/shard_map/ppermute | solution.py:32
  68.8 1.9 %collective-permute-start.24 = (bf16[112,1920]{1,0:T(8,128)(2,1)S(1)}, bf16[112,1920]{1,0:T(8,128)(2,1)S(1)}, u32[]{:S(2)}, u32[]{:S(2)}) collective-permute-start(bf16[112,1920]{1,0:T(8,128)(2,1)S(1)} %slice.69), channel_id=1, source_target_pairs={{0,24},{8,0},{16,8},{24,16},{1,25},{9,1},{17,9},{25,17},{2,26},{10... | collective-permute-start | bytes 1290248 | tf_op jit(solution)/shard_map/ppermute | solution.py:32
  71.9 3.3 %collective-permute-start.26 = (bf16[128,1920]{1,0:T(8,128)(2,1)S(1)}, bf16[128,1920]{1,0:T(8,128)(2,1)S(1)}, u32[]{:S(2)}, u32[]{:S(2)}) collective-permute-start(bf16[128,1920]{1,0:T(8,128)(2,1)S(1)} %slice.71), channel_id=1, source_target_pairs={{0,96},{32,0},{64,32},{96,64},{1,97},{33,1},{65,33},{97,65},{2,98}... | collective-permute-start | bytes 1474568 | tf_op jit(solution)/shard_map/ppermute | solution.py:32
  79.0 3.1 %collective-permute-done.25 = bf16[128,1920]{1,0:T(8,128)(2,1)S(1)} collective-permute-done((bf16[128,1920]{1,0:T(8,128)(2,1)S(1)}, bf16[128,1920]{1,0:T(8,128)(2,1)S(1)}, u32[]{:S(2)}, u32[]{:S(2)}) %collective-permute-start.25) | collective-permute-done | bytes 491552 | tf_op jit(solution)/shard_map/ppermute | solution.py:32
  93.3 1.7 %convolution_convert_fusion.1 = bf16[256,1920]{1,0:T(8,128)(2,1)} fusion(bf16[64,1920]{1,0:T(8,128)(2,1)S(1)} %get-tuple-element.191, bf16[64,1920]{1,0:T(8,128)(2,1)S(1)} %get-tuple-element.194, bf16[64,1920]{1,0:T(8,128)(2,1)S(1)} %get-tuple-element.178, bf16[64,1920]{1,0:T(8,128)(2,1)S(1)} %get-tuple-element.174, s32[256]{0:T(256)S(1)} %get-tuple-element.196, ...), kind=kOutput, calls=%fused_computation.16 | convolution fusion | flops 258244608 | bytes 1972996 | tf_op jit(solution)/shard_map/dot_general | solution.py:427
  95.0 3.8 %conditional.4 = (f32[256,240]{1,0:T(8,128)S(1)}, f32[256,240]{1,0:T(8,128)S(1)}, f32[256,240]{1,0:T(8,128)S(1)}, f32[256,240]{1,0:T(8,128)S(1)}, f32[256,240]{1...) conditional(s32[]{:T(128)} %bitcast.15, () %tuple.41, ...), branch_computations={%region_2.3_spmd, %region_3.4_spmd} | conditional | flops 1887436800 | bytes 17203264 | solution.py:450
  99.7 2.9 %code_near.2 = (s16[4,256,256]{2,1,0:T(8,128)(2,1)S(1)}, s16[4,256,256]{2,1,0:T(8,128)(2,1)S(1)}) custom-call(f32[256,240]{1,0:T(8,128)S(1)} %get-tuple-element.155.refs_0_, f32[256,240]{1,0:T(8,128)S(1)} %get-tuple-element.156.refs_1_, f32[256,240]{1,0:T(8,128)S(1)} %get-tuple-element.157.refs_2_, f32[256,240]{1,0:T(8,128)} %copy-done.31, ...), custom_call_target="tpu_custom_call" | custom-call | tf_op jit(solution)/shard_map/code_near/pallas_call | solution.py:325
  102.6 2.9 %collective-permute-start.36 = (s16[4,256,256]{2,1,0:T(8,128)(2,1)S(1)}, s16[4,256,256]{2,1,0:T(8,128)(2,1)S(1)}, u32[]{:S(2)}, u32[]{:S(2)}) collective-permute-start(s16[4,256,256]{2,1,0:T(8,128)(2,1)S(1)} %get-tuple-element.137), channel_id=1, source_target_pairs={{0,2},{2,4},{4,6},{6,0},{1,3},{3,5},{5,7},{7,1},{8,10},{10,12},{12... | collective-permute-start | bytes 1572872 | tf_op jit(solution)/shard_map/ppermute | solution.py:32
  106.2 5.4 %conditional.5 = (f32[256,240]{1,0:T(8,128)S(1)}, f32[256,240]{1,0:T(8,128)S(1)}, f32[256,240]{1,0:T(8,128)S(1)}, f32[256,240]{1,0:T(8,128)S(1)}, f32[256,240]{1...) conditional(s32[]{:T(128)} %bitcast.15, () %tuple.40, ...), branch_computations={%region_4.5_spmd, %region_5.6_spmd} | conditional | flops 1887436800 | bytes 31948976 | solution.py:450
  106.2 1.8 %fusion.57 = f32[256,240]{1,0:T(8,128)S(1)} fusion(bf16[256,1920]{1,0:T(8,128)(2,1)S(1)} %get-tuple-element.59, bf16[240,1920]{1,0:T(8,128)(2,1)} %get-tuple-element.60), kind=kOutput, calls=%fused_computation.113 | convolution fusion | flops 235929600 | bytes 2150400 | tf_op jit(solution)/shard_map/cond | solution.py:450
  111.7 1.6 %code_near.3 = (s16[4,256,256]{2,1,0:T(8,128)(2,1)S(1)}, s16[4,256,256]{2,1,0:T(8,128)(2,1)S(1)}) custom-call(f32[256,240]{1,0:T(8,128)S(1)} %get-tuple-element.163.refs_0_, f32[256,240]{1,0:T(8,128)S(1)} %get-tuple-element.164.refs_1_, f32[256,240]{1,0:T(8,128)S(1)} %get-tuple-element.165.refs_2_, f32[256,240]{1,0:T(8,128)S(1)} %get-tuple-element.166.refs_3_, ...), custom_call_target="tpu_custom_call" | custom-call | tf_op jit(solution)/shard_map/code_near/pallas_call | solution.py:325
  116.5 1.8 %collective-permute-start.35 = (s16[4,256,256]{2,1,0:T(8,128)(2,1)S(1)}, s16[4,256,256]{2,1,0:T(8,128)(2,1)S(1)}, u32[]{:S(2)}, u32[]{:S(2)}) collective-permute-start(s16[4,256,256]{2,1,0:T(8,128)(2,1)S(1)} %get-tuple-element.150), channel_id=1, source_target_pairs={{0,6},{2,0},{4,2},{6,4},{1,7},{3,1},{5,3},{7,5},{8,14},{10,8},{12,... | collective-permute-start | bytes 1572872 | tf_op jit(solution)/shard_map/ppermute | solution.py:32
  121.0 2.4 %code_last.2.refs_6_ = s16[16,8,16,256]{3,2,1,0:T(8,128)(2,1)} custom-call(f32[256,240]{1,0:T(8,128)S(1)} %fusion.77.refs_0_, f32[256,240]{1,0:T(8,128)S(1)} %fusion.78.refs_1_, f32[256,240]{1,0:T(8,128)S(1)} %fusion.79.refs_2_, f32[256,240]{1,0:T(8,128)S(1)} %fusion.80.refs_3_, s16[4,256,256]{2,1,0:T(8,128)(2,1)S(1)} %collective-permute-done.36.refs_4_.refs_6_, ...), custom_call_target="tpu_custom_call" | custom-call | tf_op jit(solution)/shard_map/code_last/pallas_call | solution.py:339
  123.4 7.2 %collective-permute-done.34.refs_4_ = s16[4,256,256]{2,1,0:T(8,128)(2,1)S(1)} collective-permute-done((s16[4,256,256]{2,1,0:T(8,128)(2,1)S(1)}, s16[4,256,256]{2,1,0:T(8,128)(2,1)S(1)}, u32[]{:S(2)}, u32[]{:S(2)}) %collective-permute-start.34) | collective-permute-done | bytes 524320 | tf_op jit(solution)/shard_map/ppermute | solution.py:32
  130.6 2.4 %code_last.3 = s16[16,8,16,256]{3,2,1,0:T(8,128)(2,1)} custom-call(f32[256,240]{1,0:T(8,128)S(1)} %fusion.73.refs_0_, f32[256,240]{1,0:T(8,128)S(1)} %fusion.74.refs_1_, f32[256,240]{1,0:T(8,128)S(1)} %fusion.75.refs_2_, f32[256,240]{1,0:T(8,128)S(1)} %fusion.76.refs_3_, ...), custom_call_target="tpu_custom_call", output_to_operand_aliasing={{}: (6, {})} | custom-call | tf_op jit(solution)/shard_map/code_last/pallas_call | solution.py:339
  133.0 6.2 %all-to-all-start = ((s16[16,8,16,256]{3,2,1,0:T(8,128)(2,1)}), s16[16,8,16,256]{3,2,1,0:T(8,128)(2,1)S(1)}, u32[]{:S(2)}, u32[]{:S(2)}) async-start(s16[16,8,16,256]{3,2,1,0:T(8,128)(2,1)} %code_last.3), calls=%async_computation | async-start | bytes 2097152 | tf_op jit(solution)/shard_map/all_to_all | solution.py:459
  141.3 2.2 %reshape.76 = s32[16,8,16,4,2]{3,2,1,0,4:T(8,128)S(1)} reshape(s32[8192,2]{0,1:T(2,128)S(1)} %copy-done.33) | data formatting | bytes 131072 | tf_op jit(solution)/shard_map/reshape | solution.py:465
  145.8 11.0 %all-to-all-done.refs_0_ = s16[16,8,16,256]{3,2,1,0:T(8,128)(2,1)S(1)} async-done(((s16[16,8,16,256]{3,2,1,0:T(8,128)(2,1)}), s16[16,8,16,256]{3,2,1,0:T(8,128)(2,1)S(1)}, u32[]{:S(2)}, u32[]{:S(2)}) %all-to-all-start) | async-done | bytes 1048608 | tf_op jit(solution)/shard_map/all_to_all | solution.py:459
  156.8 3.9 %finish.1 = f32[64,7680]{1,0:T(8,128)} custom-call(s16[16,8,16,256]{3,2,1,0:T(8,128)(2,1)S(1)} %all-to-all-done.refs_0_, f32[32,256]{1,0:T(8,128)S(1)} %pad.4.refs_1_, f32[64,1]{1,0:T(8,128)S(1)} %broadcast_in_dim.55.refs_2_), custom_call_target="tpu_custom_call" | custom-call | tf_op jit(solution)/shard_map/finish/pallas_call | solution.py:371
  (181 shorter events, 41.9 us)
Async XLA Ops:
  0.0 144.0 %copy-start = (f32[200]{0:T(256)S(1)}, f32[200]{0:T(256)}, u32[]{:S(2)}) copy-start(f32[200]{0:T(256)} %param.18) | copy-start | bytes 2404
  0.0 4.1 %collective-permute-start.12 = (bf16[480,1920]{1,0:T(8,128)(2,1)}, bf16[480,1920]{1,0:T(8,128)(2,1)}, u32[]{:S(2)}, u32[]{:S(2)}) collective-permute-start(bf16[480,1920]{1,0:T(8,128)(2,1)} %bitcast.99), channel_id=1, source_target_pairs={{0,1},{1,0},{2,3},{3,2},{4,5},{5,4},{6,7},{7,6},{8,9},{9,8},{10,11... | collective-permute-start | bytes 5529608 | tf_op jit(solution)/shard_map/ppermute | solution.py:42
  4.1 30.9 %copy-start.2 = (bf16[1,480,1920]{2,1,0:T(8,128)(2,1)S(1)}, bf16[1,480,1920]{2,1,0:T(8,128)(2,1)}, u32[]{:S(2)}) copy-start(bf16[1,480,1920]{2,1,0:T(8,128)(2,1)} %param.14) | copy-start | bytes 5529604
  8.1 11.5 %collective-permute-start.16 = (bf16[240,384]{1,0:T(8,128)(2,1)S(1)}, bf16[240,384]{1,0:T(8,128)(2,1)S(1)}, u32[]{:S(2)}, u32[]{:S(2)}) collective-permute-start(bf16[240,384]{1,0:T(8,128)(2,1)S(1)} %get-tuple-element.110.after), channel_id=1, source_target_pairs={{0,2},{2,4},{4,6},{6,0},{1,3},{3,5},{5,7},{7,1},{8,10},{10,12},{12... | collective-permute-start | bytes 552968 | tf_op jit(solution)/shard_map/ppermute | solution.py:32
  12.8 27.2 %collective-permute-start.15 = (bf16[64,1920]{1,0:T(8,128)(2,1)S(1)}, bf16[64,1920]{1,0:T(8,128)(2,1)S(1)}, u32[]{:S(2)}, u32[]{:S(2)}) collective-permute-start(bf16[64,1920]{1,0:T(8,128)(2,1)S(1)} %get-tuple-element.113), channel_id=1, source_target_pairs={{0,2},{2,4},{4,6},{6,0},{1,3},{3,5},{5,7},{7,1},{8,10},{10,12},{12... | collective-permute-start | bytes 737288 | tf_op jit(solution)/shard_map/ppermute | solution.py:32
  14.3 25.7 %collective-permute-start.14 = (bf16[64,1920]{1,0:T(8,128)(2,1)S(1)}, bf16[64,1920]{1,0:T(8,128)(2,1)S(1)}, u32[]{:S(2)}, u32[]{:S(2)}) collective-permute-start(bf16[64,1920]{1,0:T(8,128)(2,1)S(1)} %get-tuple-element.112), channel_id=1, source_target_pairs={{0,6},{2,0},{4,2},{6,4},{1,7},{3,1},{5,3},{7,5},{8,14},{10,8},{12,... | collective-permute-start | bytes 737288 | tf_op jit(solution)/shard_map/ppermute | solution.py:32
  16.1 23.9 %collective-permute-start.13 = (bf16[64,1920]{1,0:T(8,128)(2,1)S(1)}, bf16[64,1920]{1,0:T(8,128)(2,1)S(1)}, u32[]{:S(2)}, u32[]{:S(2)}) collective-permute-start(bf16[64,1920]{1,0:T(8,128)(2,1)S(1)} %get-tuple-element.111), channel_id=1, source_target_pairs={{0,4},{2,6},{4,0},{6,2},{1,5},{3,7},{5,1},{7,3},{8,12},{10,14},{12... | collective-permute-start | bytes 737288 | tf_op jit(solution)/shard_map/ppermute | solution.py:32
  17.6 14.0 %collective-permute-start.17 = (bf16[240,384]{1,0:T(8,128)(2,1)S(1)}, bf16[240,384]{1,0:T(8,128)(2,1)S(1)}, u32[]{:S(2)}, u32[]{:S(2)}) collective-permute-start(bf16[240,384]{1,0:T(8,128)(2,1)S(1)} %get-tuple-element.115), channel_id=1, source_target_pairs={{0,4},{2,6},{4,0},{6,2},{1,5},{3,7},{5,1},{7,3},{8,12},{10,14},{12... | collective-permute-start | bytes 552968 | tf_op jit(solution)/shard_map/ppermute | solution.py:32
  19.6 15.4 %collective-permute-start.18 = (bf16[240,384]{1,0:T(8,128)(2,1)S(1)}, bf16[240,384]{1,0:T(8,128)(2,1)S(1)}, u32[]{:S(2)}, u32[]{:S(2)}) collective-permute-start(bf16[240,384]{1,0:T(8,128)(2,1)S(1)} %get-tuple-element.116), channel_id=1, source_target_pairs={{0,6},{2,0},{4,2},{6,4},{1,7},{3,1},{5,3},{7,5},{8,14},{10,8},{12,... | collective-permute-start | bytes 552968 | tf_op jit(solution)/shard_map/ppermute | solution.py:32
  40.0 43.3 %copy-start.10 = (bf16[240,1920]{1,0:T(8,128)(2,1)}, bf16[240,1920]{1,0:T(8,128)(2,1)S(1)}, u32[]{:S(2)}) copy-start(bf16[240,1920]{1,0:T(8,128)(2,1)S(1)} %assemble.1) | copy-start | bytes 2764804
  40.1 27.0 %collective-permute-start.21 = (bf16[256,1920]{1,0:T(8,128)(2,1)S(1)}, bf16[256,1920]{1,0:T(8,128)(2,1)S(1)}, u32[]{:S(2)}, u32[]{:S(2)}) collective-permute-start(bf16[256,1920]{1,0:T(8,128)(2,1)S(1)} %pad_maximum_fusion), channel_id=1, source_target_pairs={{0,32},{32,64},{64,96},{96,0},{1,33},{33,65},{65,97},{97,1},{2,34}... | collective-permute-start | bytes 2949128 | tf_op jit(solution)/shard_map/ppermute | solution.py:32
  42.1 25.0 %collective-permute-start.22 = (bf16[256,1920]{1,0:T(8,128)(2,1)S(1)}, bf16[256,1920]{1,0:T(8,128)(2,1)}, u32[]{:S(2)}, u32[]{:S(2)}) collective-permute-start(bf16[256,1920]{1,0:T(8,128)(2,1)S(1)} %pad_maximum_fusion), channel_id=1, source_target_pairs={{0,96},{32,0},{64,32},{96,64},{1,97},{33,1},{65,33},{97,65},{2,98}... | collective-permute-start | bytes 2949128 | tf_op jit(solution)/shard_map/ppermute | solution.py:32
  45.0 22.1 %collective-permute-start.19 = (bf16[240,1920]{1,0:T(8,128)(2,1)S(1)}, bf16[240,1920]{1,0:T(8,128)(2,1)S(1)}, u32[]{:S(2)}, u32[]{:S(2)}) collective-permute-start(bf16[240,1920]{1,0:T(8,128)(2,1)S(1)} %assemble.1), channel_id=1, source_target_pairs={{0,8},{8,16},{16,24},{24,0},{1,9},{9,17},{17,25},{25,1},{2,10},{10... | collective-permute-start | bytes 2764808 | tf_op jit(solution)/shard_map/ppermute | solution.py:32
  46.6 20.4 %collective-permute-start.20 = (bf16[240,1920]{1,0:T(8,128)(2,1)S(1)}, bf16[240,1920]{1,0:T(8,128)(2,1)S(1)}, u32[]{:S(2)}, u32[]{:S(2)}) collective-permute-start(bf16[240,1920]{1,0:T(8,128)(2,1)S(1)} %assemble.1), channel_id=1, source_target_pairs={{0,24},{8,0},{16,8},{24,16},{1,25},{9,1},{17,9},{25,17},{2,26},{10... | collective-permute-start | bytes 2764808 | tf_op jit(solution)/shard_map/ppermute | solution.py:32
  48.3 37.6 %collective-permute-start.27 = (bf16[240,1920]{1,0:T(8,128)(2,1)S(1)}, bf16[240,1920]{1,0:T(8,128)(2,1)S(1)}, u32[]{:S(2)}, u32[]{:S(2)}) collective-permute-start(bf16[240,1920]{1,0:T(8,128)(2,1)S(1)} %assemble.1), channel_id=1, source_target_pairs={{0,1},{1,0},{2,3},{3,2},{4,5},{5,4},{6,7},{7,6},{8,9},{9,8},{10,11... | collective-permute-start | bytes 2764808 | tf_op jit(solution)/shard_map/ppermute | solution.py:42
  67.0 17.8 %copy-start.13 = (bf16[240,1920]{1,0:T(8,128)(2,1)}, bf16[240,1920]{1,0:T(8,128)(2,1)S(1)}, u32[]{:S(2)}) copy-start(bf16[240,1920]{1,0:T(8,128)(2,1)S(1)} %collective-permute-done.19) | copy-start | bytes 2764804
  67.0 28.0 %copy-start.22 = (bf16[240,1920]{1,0:T(8,128)(2,1)}, bf16[240,1920]{1,0:T(8,128)(2,1)S(1)}, u32[]{:S(2)}) copy-start(bf16[240,1920]{1,0:T(8,128)(2,1)S(1)} %collective-permute-done.20) | copy-start | bytes 2764804
  67.1 11.9 %collective-permute-start.23 = (bf16[128,1920]{1,0:T(8,128)(2,1)S(1)}, bf16[128,1920]{1,0:T(8,128)(2,1)S(1)}, u32[]{:S(2)}, u32[]{:S(2)}) collective-permute-start(bf16[128,1920]{1,0:T(8,128)(2,1)S(1)} %slice.68), channel_id=1, source_target_pairs={{0,8},{8,16},{16,24},{24,0},{1,9},{9,17},{17,25},{25,1},{2,10},{10... | collective-permute-start | bytes 1474568 | tf_op jit(solution)/shard_map/ppermute | solution.py:32
  68.8 9.1 %collective-permute-start.24 = (bf16[112,1920]{1,0:T(8,128)(2,1)S(1)}, bf16[112,1920]{1,0:T(8,128)(2,1)S(1)}, u32[]{:S(2)}, u32[]{:S(2)}) collective-permute-start(bf16[112,1920]{1,0:T(8,128)(2,1)S(1)} %slice.69), channel_id=1, source_target_pairs={{0,24},{8,0},{16,8},{24,16},{1,25},{9,1},{17,9},{25,17},{2,26},{10... | collective-permute-start | bytes 1290248 | tf_op jit(solution)/shard_map/ppermute | solution.py:32
  70.7 11.4 %collective-permute-start.25 = (bf16[128,1920]{1,0:T(8,128)(2,1)S(1)}, bf16[128,1920]{1,0:T(8,128)(2,1)S(1)}, u32[]{:S(2)}, u32[]{:S(2)}) collective-permute-start(bf16[128,1920]{1,0:T(8,128)(2,1)S(1)} %slice.70), channel_id=1, source_target_pairs={{0,32},{32,64},{64,96},{96,0},{1,33},{33,65},{65,97},{97,1},{2,34}... | collective-permute-start | bytes 1474568 | tf_op jit(solution)/shard_map/ppermute | solution.py:32
  71.9 10.6 %collective-permute-start.26 = (bf16[128,1920]{1,0:T(8,128)(2,1)S(1)}, bf16[128,1920]{1,0:T(8,128)(2,1)S(1)}, u32[]{:S(2)}, u32[]{:S(2)}) collective-permute-start(bf16[128,1920]{1,0:T(8,128)(2,1)S(1)} %slice.71), channel_id=1, source_target_pairs={{0,96},{32,0},{64,32},{96,64},{1,97},{33,1},{65,33},{97,65},{2,98}... | collective-permute-start | bytes 1474568 | tf_op jit(solution)/shard_map/ppermute | solution.py:32
  77.8 9.3 %collective-permute-start.28 = (bf16[240,1920]{1,0:T(8,128)(2,1)S(1)}, bf16[240,1920]{1,0:T(8,128)(2,1)S(1)}, u32[]{:S(2)}, u32[]{:S(2)}) collective-permute-start(bf16[240,1920]{1,0:T(8,128)(2,1)S(1)} %collective-permute-done.20), channel_id=1, source_target_pairs={{0,1},{1,0},{2,3},{3,2},{4,5},{5,4},{6,7},{7,6},{8,9},{9,8},{10,11... | collective-permute-start | bytes 2764808 | tf_op jit(solution)/shard_map/ppermute | solution.py:42
  79.0 10.7 %collective-permute-start.31 = (bf16[240,1920]{1,0:T(8,128)(2,1)S(1)}, bf16[240,1920]{1,0:T(8,128)(2,1)S(1)}, u32[]{:S(2)}, u32[]{:S(2)}) collective-permute-start(bf16[240,1920]{1,0:T(8,128)(2,1)S(1)} %collective-permute-done.19), channel_id=1, source_target_pairs={{0,1},{1,0},{2,3},{3,2},{4,5},{5,4},{6,7},{7,6},{8,9},{9,8},{10,11... | collective-permute-start | bytes 2764808 | tf_op jit(solution)/shard_map/ppermute | solution.py:42
  84.2 5.9 %collective-permute-start.29 = (bf16[128,1920]{1,0:T(8,128)(2,1)S(1)}, bf16[128,1920]{1,0:T(8,128)(2,1)S(1)}, u32[]{:S(2)}, u32[]{:S(2)}) collective-permute-start(bf16[128,1920]{1,0:T(8,128)(2,1)S(1)} %collective-permute-done.23), channel_id=1, source_target_pairs={{0,1},{1,0},{2,3},{3,2},{4,5},{5,4},{6,7},{7,6},{8,9},{9,8},{10,11... | collective-permute-start | bytes 1474568 | tf_op jit(solution)/shard_map/ppermute | solution.py:42
  84.3 5.9 %collective-permute-start.30 = (bf16[112,1920]{1,0:T(8,128)(2,1)S(1)}, bf16[112,1920]{1,0:T(8,128)(2,1)S(1)}, u32[]{:S(2)}, u32[]{:S(2)}) collective-permute-start(bf16[112,1920]{1,0:T(8,128)(2,1)S(1)} %collective-permute-done.24), channel_id=1, source_target_pairs={{0,1},{1,0},{2,3},{3,2},{4,5},{5,4},{6,7},{7,6},{8,9},{9,8},{10,11... | collective-permute-start | bytes 1290248 | tf_op jit(solution)/shard_map/ppermute | solution.py:42
  88.5 10.5 %collective-permute-start.32 = (s16[4,256,256]{2,1,0:T(8,128)(2,1)S(1)}, s16[4,256,256]{2,1,0:T(8,128)(2,1)S(1)}, u32[]{:S(2)}, u32[]{:S(2)}) collective-permute-start(s16[4,256,256]{2,1,0:T(8,128)(2,1)S(1)} %code_far.2), channel_id=1, source_target_pairs={{0,2},{1,7},{2,4},{3,1},{4,6},{5,3},{6,0},{7,5},{8,10},{9,15},{10,... | collective-permute-start | bytes 1572872 | tf_op jit(solution)/shard_map/ppermute | solution.py:38
  92.0 19.6 %collective-permute-start.33 = (s16[4,256,256]{2,1,0:T(8,128)(2,1)S(1)}, s16[4,256,256]{2,1,0:T(8,128)(2,1)S(1)}, u32[]{:S(2)}, u32[]{:S(2)}) collective-permute-start(s16[4,256,256]{2,1,0:T(8,128)(2,1)S(1)} %code_far.3), channel_id=1, source_target_pairs={{0,2},{1,7},{2,4},{3,1},{4,6},{5,3},{6,0},{7,5},{8,10},{9,15},{10,... | collective-permute-start | bytes 1572872 | tf_op jit(solution)/shard_map/ppermute | solution.py:38
  102.6 18.4 %collective-permute-start.36 = (s16[4,256,256]{2,1,0:T(8,128)(2,1)S(1)}, s16[4,256,256]{2,1,0:T(8,128)(2,1)S(1)}, u32[]{:S(2)}, u32[]{:S(2)}) collective-permute-start(s16[4,256,256]{2,1,0:T(8,128)(2,1)S(1)} %get-tuple-element.137), channel_id=1, source_target_pairs={{0,2},{2,4},{4,6},{6,0},{1,3},{3,5},{5,7},{7,1},{8,10},{10,12},{12... | collective-permute-start | bytes 1572872 | tf_op jit(solution)/shard_map/ppermute | solution.py:32
  105.6 15.4 %collective-permute-start.37 = (s16[4,256,256]{2,1,0:T(8,128)(2,1)S(1)}, s16[4,256,256]{2,1,0:T(8,128)(2,1)S(1)}, u32[]{:S(2)}, u32[]{:S(2)}) collective-permute-start(s16[4,256,256]{2,1,0:T(8,128)(2,1)S(1)} %get-tuple-element.138), channel_id=1, source_target_pairs={{0,6},{2,0},{4,2},{6,4},{1,7},{3,1},{5,3},{7,5},{8,14},{10,8},{12,... | collective-permute-start | bytes 1572872 | tf_op jit(solution)/shard_map/ppermute | solution.py:32
  115.0 15.6 %collective-permute-start.34 = (s16[4,256,256]{2,1,0:T(8,128)(2,1)S(1)}, s16[4,256,256]{2,1,0:T(8,128)(2,1)S(1)}, u32[]{:S(2)}, u32[]{:S(2)}) collective-permute-start(s16[4,256,256]{2,1,0:T(8,128)(2,1)S(1)} %get-tuple-element.149), channel_id=1, source_target_pairs={{0,2},{2,4},{4,6},{6,0},{1,3},{3,5},{5,7},{7,1},{8,10},{10,12},{12... | collective-permute-start | bytes 1572872 | tf_op jit(solution)/shard_map/ppermute | solution.py:32
  116.5 14.1 %collective-permute-start.35 = (s16[4,256,256]{2,1,0:T(8,128)(2,1)S(1)}, s16[4,256,256]{2,1,0:T(8,128)(2,1)S(1)}, u32[]{:S(2)}, u32[]{:S(2)}) collective-permute-start(s16[4,256,256]{2,1,0:T(8,128)(2,1)S(1)} %get-tuple-element.150), channel_id=1, source_target_pairs={{0,6},{2,0},{4,2},{6,4},{1,7},{3,1},{5,3},{7,5},{8,14},{10,8},{12,... | collective-permute-start | bytes 1572872 | tf_op jit(solution)/shard_map/ppermute | solution.py:32
  133.0 23.8 %all-to-all-start = ((s16[16,8,16,256]{3,2,1,0:T(8,128)(2,1)}), s16[16,8,16,256]{3,2,1,0:T(8,128)(2,1)S(1)}, u32[]{:S(2)}, u32[]{:S(2)}) async-start(s16[16,8,16,256]{3,2,1,0:T(8,128)(2,1)} %code_last.3), calls=%async_computation | async-start | bytes 2097152 | tf_op jit(solution)/shard_map/all_to_all | solution.py:459
  (29 other events, 106.2 us)
